TPU v7x, 256 devices: a whole 4x4x8 slice. The times are simulated.
256 devices in a mesh: prow: 32 (over x, z), pcol: 8 (over y, core).
Axes of the slice: x: 4, y: 4, z: 8, core: 2. Of those that a mesh axis runs over, the one named last changes fastest.
Arguments:
- matrix: bfloat16 [32, 3, 256, 8, 12, 256], P('prow', None, None, 'pcol')
- row_perm: int32 [32, 3, 256], P('prow'), may hold values from 0 to 255, as said below
- block_pattern: int32 [96, 96], replicated, may hold values from 0 to 1, as said below
Outputs:
- factored: bfloat16 [32, 3, 256, 8, 12, 256], P('prow', None, None, 'pcol')
Inputs may be any that keep to these rules, and one draw needn't show every extreme that they name: `row_perm`: each row of 256 entries along the last dimension is a permutation of 0 to 255. `block_pattern`: 0 or 1. Diagonal blocks are 1 and block (1, 0) is 0. The pattern is closed under the fill of supernodes 0 and 1: if (i, k) and (k, j) are 1 with i > k and j > k, then (i, j) is 1 (for k = 1 after the fill of k = 0). For k = 0 and k = 1, the blocks (k, j) with j >= k that lie in one process-grid column (j % 8 fixed) hold at most 6 ones, and exactly 6 in some process-grid column.
All inputs are finite; a program needn't handle non-finite values.
Results may differ from a plain program's by a relative error of at most 0.0028.
Values may be sent and summed in bfloat16 or wider, within the bound.
No kernel may reach another device: no remote copies, remote signals or barrier semaphores. Data moves between devices by JAX's collectives and lax.ppermute only.
A program may use at most 128 MiB of HBM per device.

v0:
```python
import jax
import jax.numpy as jnp
from jax import lax
from jax.sharding import PartitionSpec as P

NEWTON = 3


def from_root(value, axis, source):
    kept = jnp.where(lax.axis_index(axis) == source, value, 0).astype(value.dtype)
    return lax.psum(kept, axis)


def newton_inverse(diagonal_block):
    pivots = jnp.diagonal(diagonal_block)
    inverse = jnp.diag(1.0 / pivots)
    identity = jnp.eye(diagonal_block.shape[0], dtype=jnp.float32)
    for sweep_index in range(NEWTON):
        product = jnp.dot(diagonal_block, inverse, precision=lax.Precision.HIGHEST)
        inverse = jnp.dot(inverse, 2.0 * identity - product, precision=lax.Precision.HIGHEST)
    return inverse


def send_upper(current, supernode):
    rows_grid = lax.axis_size("prow")
    owner_row = supernode % rows_grid
    own_row = current[supernode // rows_grid]
    upper_row = from_root(own_row, "prow", owner_row)
    return upper_row


def panels(current, upper_row, supernode):
    rows_grid = lax.axis_size("prow")
    cols_grid = lax.axis_size("pcol")
    grid_row = lax.axis_index("prow")
    grid_col = lax.axis_index("pcol")
    local_rows = current.shape[0]
    local_cols = current.shape[2]
    row_numbers = jnp.arange(local_rows) * rows_grid + grid_row
    col_numbers = jnp.arange(local_cols) * cols_grid + grid_col
    owner_col = supernode % cols_grid
    local_col = supernode // cols_grid
    inverse = newton_inverse(upper_row[:, local_col, :].astype(jnp.float32))
    upper_used = jnp.where(
        (col_numbers > supernode)[None, :, None], upper_row, jnp.zeros_like(upper_row)
    )
    column = current[:, :, local_col, :]
    own_lower = jnp.einsum(
        "trb,bc->trc", column.astype(jnp.float32), inverse, precision=lax.Precision.HIGHEST
    ).astype(jnp.bfloat16)
    own_lower = jnp.where(
        (row_numbers > supernode)[:, None, None], own_lower, jnp.zeros_like(own_lower)
    )
    lower_col = from_root(own_lower, "pcol", owner_col)
    return (upper_used, lower_col, own_lower)


def store_lower(current, own_lower, supernode):
    rows_grid = lax.axis_size("prow")
    cols_grid = lax.axis_size("pcol")
    grid_row = lax.axis_index("prow")
    grid_col = lax.axis_index("pcol")
    row_numbers = jnp.arange(current.shape[0]) * rows_grid + grid_row
    keep_mask = ((grid_col == supernode % cols_grid) & (row_numbers > supernode))[:, None, None]
    local_col = supernode // cols_grid
    return current.at[:, :, local_col, :].set(
        jnp.where(keep_mask, own_lower, current[:, :, local_col, :])
    )


def schur(target, lower_col, upper_used):
    product = jnp.einsum("tra,auc->truc", lower_col, upper_used, preferred_element_type=jnp.float32)
    return (target.astype(jnp.float32) - product).astype(jnp.bfloat16)


def local(matrix, row_perm, block_pattern):
    rows_grid = lax.axis_size("prow")
    cols_grid = lax.axis_size("pcol")
    grid_row = lax.axis_index("prow")
    grid_col = lax.axis_index("pcol")
    local_blocks = matrix[0, :, :, 0, :, :]
    local_rows = local_blocks.shape[0]
    local_cols = local_blocks.shape[2]
    current = jax.vmap(lambda block_row, row_order: block_row[row_order])(local_blocks, row_perm[0])
    grid_pattern = block_pattern.reshape(local_rows, rows_grid, local_cols, cols_grid)
    own_pattern = lax.dynamic_index_in_dim(grid_pattern, grid_row, 1, keepdims=False)
    own_pattern = lax.dynamic_index_in_dim(own_pattern, grid_col, 2, keepdims=False)
    current = current * own_pattern[:, None, :, None].astype(jnp.bfloat16)
    for supernode in range(2):
        upper_used, lower_col, own_lower = panels(
            current, send_upper(current, supernode), supernode
        )
        current = store_lower(schur(current, lower_col, upper_used), own_lower, supernode)
    return current.reshape(matrix.shape)


def solution(mesh):
    placed = (P("prow", None, None, "pcol", None, None), P("prow", None, None), P())
    return jax.shard_map(
        local,
        mesh=mesh,
        in_specs=placed,
        out_specs=P("prow", None, None, "pcol", None, None),
        check_vma=False,
    )
```

profile of v0, /device:TPU:2, one launch (start us, length us, event | category | flops | bytes accessed | tf_op | source)
XLA Modules:
  0.0 508.9 jit_solution(12403247828440862597)
XLA Ops:
  6.5 0.9 copy.25
  7.9 8.0 %copy.39 = bf16[1,3,256,1,12,256]{5,4,2,1,3,0:T(8,128)(2,1)} copy(bf16[1,3,256,1,12,256]{5,2,4,3,1,0:T(8,128)(2,1)} %param.7) | data formatting | bytes 9437184 | tf_op args[0]
  15.9 9.6 %gather_fusion.2 = bf16[768,12,256]{2,1,0:T(8,128)(2,1)} fusion(bf16[3,256,12,256]{3,2,1,0:T(8,128)(2,1)} %bitcast.105, s32[768]{0:T(1024)S(1)} %reshape.164), kind=kCustom, calls=%fused_computation.2 | custom fusion | bytes 9443328 | tf_op jit(solution)/shard_map/vmap()/gather | solution.py:84
  25.4 4.4 copy.24
  30.3 2.2 copy-done
  32.4 1.3 fusion.1
  33.8 153.4 %all-reduce.5.cloned.1.call-done = bf16[256,12,256]{2,0,1:T(8,128)(2,1)} async-done(((bf16[256,12,256]{2,0,1:T(8,128)(2,1)}), bf16[256,12,256]{2,0,1:T(8,128)(2,1)}) %all-reduce.5.cloned.1.call-update) | async-done | bytes 1572880 | tf_op jit(solution)/shard_map/psum | solution.py:11
  187.2 1.0 fusion.32
  188.3 2.3 gather_fusion
  190.7 1.3 convolution_subtract_fusion.5
  191.9 0.4 fusion.21
  192.3 1.2 convolution_subtract_fusion.4
  193.9 1.2 convolution_subtract_fusion.3
  195.5 2.3 broadcast_select_fusion.1
  198.1 63.6 %all-reduce.7.cloned.1.call-done = bf16[3,256,256]{2,1,0:T(8,128)(2,1)} async-done(((bf16[3,256,256]{2,1,0:T(8,128)(2,1)}), bf16[3,256,256]{2,1,0:T(8,128)(2,1)}) %all-reduce.7.cloned.1.call-update) | async-done | bytes 393232 | tf_op jit(solution)/shard_map/psum | solution.py:11
  261.7 4.0 subtract_convert_fusion.1
  265.6 0.5 copy.30
  266.1 1.6 copy-done.1
  268.0 2.2 copy-done.2
  270.1 1.3 fusion
  271.5 149.7 %all-reduce.9.cloned.1.call-done = bf16[256,12,256]{2,0,1:T(8,128)(2,1)} async-done(((bf16[256,12,256]{2,0,1:T(8,128)(2,1)}), bf16[256,12,256]{2,0,1:T(8,128)(2,1)}) %all-reduce.9.cloned.1.call-update) | async-done | bytes 1572880 | tf_op jit(solution)/shard_map/psum | solution.py:11
  421.2 1.0 fusion.33
  422.2 2.3 gather_fusion.1
  424.6 1.3 convolution_subtract_fusion.2
  425.8 0.4 fusion.18
  426.3 1.2 convolution_subtract_fusion.1
  427.9 1.2 convolution_subtract_fusion
  429.5 2.3 broadcast_select_fusion
  431.8 63.8 %all-reduce.11.cloned.1.call-done = bf16[3,256,256]{2,1,0:T(8,128)(2,1)} async-done(((bf16[3,256,256]{2,1,0:T(8,128)(2,1)}), bf16[3,256,256]{2,1,0:T(8,128)(2,1)}) %all-reduce.11.cloned.1.call-update) | async-done | bytes 393232 | tf_op jit(solution)/shard_map/psum | solution.py:11
  495.5 4.0 subtract_convert_fusion
  499.5 0.5 copy.45
  500.2 2.2 copy-done.4
  (41 shorter events, 3.2 us)
Async XLA Ops:
  6.5 180.7 %all-reduce.5.cloned.1.call-start = ((), (), s32[]{:S(2)}) async-start(), calls=%async_computation | async-start | bytes 3145728 | tf_op jit(solution)/shard_map/psum | solution.py:11
  7.9 8.0 %copy-start.6 = (s32[1,3,256]{2,0,1:T(1,128)S(1)}, s32[1,3,256]{2,0,1:T(1,128)}, u32[]{:S(2)}) copy-start(s32[1,3,256]{2,0,1:T(1,128)} %param.8) | copy-start | bytes 9220
  30.2 2.2 copy-start
  33.7 227.9 %all-reduce.7.cloned.1.call-start = ((), (), s32[]{:S(2)}) async-start(), calls=%async_computation.1 | async-start | bytes 786432 | tf_op jit(solution)/shard_map/psum | solution.py:11
  187.2 74.4 %copy-start.3 = (bf16[256,12,256]{2,0,1:T(8,128)(2,1)S(1)}, bf16[256,12,256]{2,0,1:T(8,128)(2,1)}, u32[]{:S(2)}) copy-start(bf16[256,12,256]{2,0,1:T(8,128)(2,1)} %all-reduce.5.cloned.1.call-done) | copy-start | bytes 4718596
  197.9 223.3 %all-reduce.9.cloned.1.call-start = ((), (), s32[]{:S(2)}) async-start(), calls=%async_computation.2 | async-start | bytes 3145728 | tf_op jit(solution)/shard_map/psum | solution.py:11
  265.6 2.1 copy-start.1
  268.0 2.2 copy-start.2
  271.4 224.1 %all-reduce.11.cloned.1.call-start = ((), (), s32[]{:S(2)}) async-start(), calls=%async_computation.3 | async-start | bytes 786432 | tf_op jit(solution)/shard_map/psum | solution.py:11
  421.2 74.4 %copy-start.5 = (bf16[256,12,256]{2,0,1:T(8,128)(2,1)S(1)}, bf16[256,12,256]{2,0,1:T(8,128)(2,1)}, u32[]{:S(2)}) copy-start(bf16[256,12,256]{2,0,1:T(8,128)(2,1)} %all-reduce.9.cloned.1.call-done) | copy-start | bytes 4718596
  500.2 2.2 copy-start.4
Sparse Core Ops, SparseCore 0:
  33.8 153.3 all-reduce.4
  198.0 63.6 all-reduce.6
  271.5 149.5 all-reduce.8
  431.9 63.6 all-reduce.10
where the time goes:
time: 509 us
  waiting for transfers between devices  430 us (84%)
  local copies, waits for them, and re-layouts  37.1 us (7%)
  matrix products  22.1 us (4%)
  between operations  13.4 us (3%)
  other arithmetic  5.46 us (1%)
    psum x4, waiting for transfers between devices, from_root(): return lax.psum(kept, axis)  430 us
    unnamed x18, local copies, waits for them, and re-layouts  17.6 us
    gather x3, local copies, waits for them, and re-layouts, local(): block_row[row_order]  14 us
  transfers between devices with their start and end apart: 4, of which 4 were waited for; matrix products, arithmetic and copies ran while one was open for 0% of the time, Pallas kernels for 0%

commit v1 on v0

v1 whole, which is shorter than its diff:
```python
import functools

import jax
import jax.numpy as jnp
from jax import lax
from jax.experimental import pallas as pl
from jax.experimental.pallas import tpu as pltpu
from jax.sharding import PartitionSpec as P

B = 256
LR = 3
LC = 12
UCAP = 6
NEWTON = 3
ROWS_GRID = 32
COLS_GRID = 8
NX = 4
NZ = 8
PIECE = B // NX
MIB = 1 << 20

F32 = jnp.float32
BF16 = jnp.bfloat16

FAR_UP = [(0, 3), (1, 4)]
FAR_DOWN = [(0, 5), (1, 6)]
NEAR_UP = [(0, 1), (3, 4), (5, 6), (1, 2), (4, 5), (6, 7)]
NEAR_DOWN = [(0, 7), (3, 2), (1, 0), (4, 3)]
FROM_0 = "hudhuhud"
FROM_1 = "dhudhuhu"


def one_hot_rows(order):
    source = lax.broadcasted_iota(jnp.int32, (B, B), 0)
    return jnp.where(source == order, 1.0, 0.0).T.astype(BF16)


def split(value, parts):
    out = []
    for _ in range(parts):
        head = value.astype(BF16)
        out.append(head)
        value = value - head.astype(F32)
    return out


def dot(a, b):
    return jnp.dot(a, b, preferred_element_type=F32)


def pack_kernel(pattern_ref, order_ref, blocks_ref, packed_ref, first_ref):
    supernode = jnp.minimum(lax.axis_index("prow"), 1)
    grid_col = lax.axis_index("pcol")
    pick = one_hot_rows(order_ref[0:1, :])
    first = dot(pick, blocks_ref[0, 0])
    present = pattern_ref[supernode, grid_col] != 0
    first_ref[...] = jnp.where(present, first, 0.0).astype(BF16)
    slot = jnp.int32(0)
    for u in range(LC):
        col = grid_col + u * COLS_GRID
        used = (pattern_ref[supernode, col] != 0) & (col > supernode)

        @pl.when(used)
        def _(u=u, slot=slot):
            block = dot(pick, blocks_ref[0, u]).astype(BF16)
            for piece in range(NX):
                packed_ref[piece, slot] = block[piece * PIECE : (piece + 1) * PIECE]

        slot = slot + used.astype(jnp.int32)


def permute_kernel(pattern_ref, order_ref, blocks_ref, out_ref):
    t = pl.program_id(0)
    row = t * ROWS_GRID + lax.axis_index("prow")
    grid_col = lax.axis_index("pcol")
    pick = one_hot_rows(order_ref[pl.ds(t, 1), :])
    for u in range(LC):
        present = pattern_ref[row, grid_col + u * COLS_GRID] != 0

        @pl.when(present)
        def _(u=u):
            out_ref[0, u] = dot(pick, blocks_ref[0, u]).astype(BF16)

        @pl.when(jnp.logical_not(present))
        def _(u=u):
            out_ref[0, u] = jnp.zeros((B, B), BF16)


def inverse_kernel(held_ref, up_ref, down_ref, column_ref, lower_ref, first_ref, high_ref, low_ref):
    grid_row = lax.axis_index("prow")
    grid_col = lax.axis_index("pcol")
    z = grid_row % NZ

    def chosen(table):
        def of(letter, ref):
            hit = functools.reduce(jnp.logical_or, [z == i for i in range(NZ) if table[i] == letter])
            return hit, ref

        (held, h), (up, u) = of("h", held_ref), of("u", up_ref)
        return jnp.where(
            held, h[...].astype(F32), jnp.where(up, u[...].astype(F32), down_ref[...].astype(F32))
        )

    @pl.when(grid_col < 2)
    def _():
        first = chosen(FROM_0)
        first_ref[...] = first.astype(BF16)
        block = jnp.where(grid_col == 0, first, chosen(FROM_1))
        diagonal = lax.broadcasted_iota(jnp.int32, (B, B), 0) == lax.broadcasted_iota(jnp.int32, (B, B), 1)
        pivots = jnp.where(diagonal, block, 0.0)
        by_col = 1.0 / jnp.sum(pivots, axis=0, keepdims=True)
        by_row = 1.0 / jnp.sum(pivots, axis=1, keepdims=True)
        twice = jnp.where(diagonal, 2.0, 0.0)
        inverse = by_row * (twice - block * by_col)
        block16 = block.astype(BF16)
        for _ in range(NEWTON - 1):
            high, middle, low = split(inverse, 3)
            rest = twice - (dot(block16, high) + (dot(block16, middle) + dot(block16, low)))
            rest_high, rest_low = split(rest, 2)
            inverse = dot(high, rest_high) + (dot(high, rest_low) + dot(middle, rest_high))
        high, low = split(inverse, 2)
        high_ref[...] = high
        low_ref[...] = low
        for t in range(LR):
            column = column_ref[t, 0]
            lower = dot(column, high) + dot(column, low)
            lower_ref[t] = jnp.where(t * ROWS_GRID + grid_row > 0, lower, 0.0).astype(BF16)


def second_kernel(lower_ref, first_ref, high_ref, low_ref, column_ref, out_ref):
    grid_row = lax.axis_index("prow")

    @pl.when(lax.axis_index("pcol") == 1)
    def _():
        for t in range(LR):
            column = (column_ref[t, 0].astype(F32) - dot(lower_ref[t], first_ref[...])).astype(BF16)
            lower = dot(column, high_ref[...]) + dot(column, low_ref[...])
            out_ref[t] = jnp.where(t * ROWS_GRID + grid_row > 1, lower, 0.0).astype(BF16)


def schur_kernel(
    pattern_ref, own_ref, one_ref, two_ref, three_ref, low0e_ref, low0o_ref, low1e_ref, low1o_ref, in_ref, out_ref,
    upper, lower, work, upper_sem, lower_sem, in_sem, out_sem,
):
    del in_ref
    grid_row = lax.axis_index("prow")
    grid_col = lax.axis_index("pcol")
    x = grid_row // NZ

    def plan(u):
        col = grid_col + u * COLS_GRID
        use0 = (pattern_ref[0, col] != 0) & (col > 0)
        use1 = (pattern_ref[1, col] != 0) & (col > 1)
        return use0, use1, use0 | use1 | (col < 2)

    def fetch(u):
        return pltpu.make_async_copy(out_ref.at[:, u], work.at[u], in_sem.at[u])

    def store(u):
        return pltpu.make_async_copy(work.at[u], out_ref.at[:, u], out_sem.at[u])

    lowers = [
        [pltpu.make_async_copy(src, lower.at[k], lower_sem.at[k]) for k, src in enumerate(pair)]
        for pair in ((low0e_ref, low1e_ref), (low0o_ref, low1o_ref))
    ]
    for parity in range(2):

        @pl.when(grid_col % 2 == parity)
        def _(parity=parity):
            for copy in lowers[parity]:
                copy.start()

    uppers = []
    for shift, ref in enumerate((own_ref, one_ref, two_ref, three_ref)):
        rows = pl.ds(pl.multiple_of((x + NX - shift) % NX * PIECE, PIECE), PIECE)
        uppers.append(pltpu.make_async_copy(ref, upper.at[:, :, rows, :], upper_sem.at[shift]))
    for copy in uppers:
        copy.start()

    def start_fetch(u, carry):
        @pl.when(plan(u)[2])
        def _():
            fetch(u).start()

        return carry

    lax.fori_loop(0, LC, start_fetch, 0)
    for parity in range(2):

        @pl.when(grid_col % 2 == parity)
        def _(parity=parity):
            for copy in lowers[parity]:
                copy.wait()

    for copy in uppers:
        copy.wait()

    def step(u, slots):
        use0, use1, touched = plan(u)
        slot0, slot1 = slots

        @pl.when(touched)
        def _():
            fetch(u).wait()

            def update(k, slot):
                for t in range(LR):
                    product = dot(lower[k, t], upper[k, slot])
                    work[u, t] = (work[u, t].astype(F32) - product).astype(BF16)

            @pl.when(use0)
            def _():
                update(0, slot0)

            @pl.when(use1)
            def _():
                update(1, slot1)

            for k in range(2):

                @pl.when((u == 0) & (grid_col == k))
                def _(k=k):
                    for t in range(LR):

                        @pl.when(t * ROWS_GRID + grid_row > k)
                        def _(t=t):
                            work[0, t] = lower[k, t]

            store(u).start()

        return slot0 + use0.astype(jnp.int32), slot1 + use1.astype(jnp.int32)

    lax.fori_loop(0, LC, step, (jnp.int32(0), jnp.int32(0)))

    def finish(u, carry):
        @pl.when(plan(u)[2])
        def _():
            store(u).wait()

        return carry

    lax.fori_loop(0, LC, finish, 0)


def pick_by(index, options):
    value = None
    for i, option in enumerate(options):
        if option is not None:
            value = option if value is None else jnp.where(index == i, option, value)
    return value


def along_z(pairs, cols):
    rows = [(x * NZ + a, x * NZ + b) for x in range(NX) for a, b in pairs]
    if cols is None:
        return rows
    return [(a * COLS_GRID + c, b * COLS_GRID + c) for a, b in rows for c in cols]


def from_x0(shift, cols):
    rows = [(z, shift * NZ + z) for z in range(2)]
    if cols is None:
        return rows
    return [(a * COLS_GRID + c, b * COLS_GRID + c) for a, b in rows for c in cols]


def spread(sent, x, z, cols):
    axes = "prow" if cols is None else ("prow", "pcol")
    got = [sent[0]] + [lax.ppermute(sent[d], axes, from_x0(d, cols)) for d in range(1, NX)]
    mine = pick_by(x, got)
    far_up = lax.ppermute(mine, axes, along_z(FAR_UP, cols))
    far_down = lax.ppermute(mine, axes, along_z(FAR_DOWN, cols))
    held = pick_by(z, [mine, None, None, far_up, far_up, far_down, far_down, None])
    up = lax.ppermute(held, axes, along_z(NEAR_UP, cols))
    down = lax.ppermute(held, axes, along_z(NEAR_DOWN, cols))
    return held, up, down


def vmem():
    return pl.BlockSpec(memory_space=pltpu.VMEM)


def smem():
    return pl.BlockSpec(memory_space=pltpu.SMEM)


def anywhere():
    return pl.BlockSpec(memory_space=pl.ANY)


def like(*shape):
    return jax.ShapeDtypeStruct(shape, BF16)


def params(limit):
    return pltpu.CompilerParams(vmem_limit_bytes=limit * MIB)


def cost(flops, moved):
    return pl.CostEstimate(flops=flops, bytes_accessed=moved, transcendentals=0)


def local(matrix, row_perm, block_pattern):
    grid_row = lax.axis_index("prow")
    grid_col = lax.axis_index("pcol")
    x, z = grid_row // NZ, grid_row % NZ
    blocks = jnp.transpose(matrix[0, :, :, 0], (0, 2, 1, 3))
    orders = row_perm[0]
    block = B * B * 2

    packed, first = pl.pallas_call(
        pack_kernel,
        out_shape=(like(NX, UCAP, PIECE, B), like(B, B)),
        grid=(1,),
        in_specs=[smem(), vmem(), pl.BlockSpec((1, LC, B, B), lambda i: (0, 0, 0, 0))],
        out_specs=(vmem(), vmem()),
        compiler_params=params(16),
        cost_estimate=cost(2 * 7 * B**3, 19 * block),
        name="pack",
    )(block_pattern, orders, blocks)

    column_shape = pl.BlockSpec((LR, 1, B, B), lambda i: (0, 0, 0, 0))
    early = spread([first] * NX, x, z, (0, 1))
    upper = spread([packed[d] for d in range(NX)], x, z, None)

    current = pl.pallas_call(
        permute_kernel,
        out_shape=like(LR, LC, B, B),
        grid=(LR,),
        in_specs=[smem(), vmem(), pl.BlockSpec((1, LC, B, B), lambda t: (t, 0, 0, 0))],
        out_specs=pl.BlockSpec((1, LC, B, B), lambda t: (t, 0, 0, 0)),
        compiler_params=params(24),
        cost_estimate=cost(2 * LR * LC * B**3, 2 * LR * LC * block),
        name="permute",
    )(block_pattern, orders, blocks)

    lower0, first0, high, low = pl.pallas_call(
        inverse_kernel,
        out_shape=(like(LR, B, B), like(B, B), like(B, B), like(B, B)),
        grid=(1,),
        in_specs=[vmem(), vmem(), vmem(), column_shape],
        out_specs=(vmem(), vmem(), vmem(), vmem()),
        compiler_params=params(16),
        cost_estimate=cost(2 * 18 * B**3, 12 * block),
        name="inverse",
    )(*early, current)

    neighbour0 = lax.ppermute(lower0, "pcol", [(0, 1)])
    lower1 = pl.pallas_call(
        second_kernel,
        out_shape=like(LR, B, B),
        grid=(1,),
        in_specs=[vmem(), vmem(), vmem(), vmem(), column_shape],
        out_specs=vmem(),
        compiler_params=params(16),
        cost_estimate=cost(2 * 9 * B**3, 12 * block),
        name="second",
    )(neighbour0, first0, high, low, current)

    def along_y(lower, core):
        got = [lower] + [lax.ppermute(lower, "pcol", [(core, 2 * d + core)]) for d in range(1, COLS_GRID // 2)]
        return pick_by(grid_col // 2, got)

    lower0_even = along_y(lower0, 0)
    lower0_odd = lax.ppermute(lower0_even, "pcol", [(c, c + 1) for c in range(0, COLS_GRID, 2)])
    lower1_odd = along_y(lower1, 1)
    lower1_even = lax.ppermute(lower1_odd, "pcol", [(c + 1, c) for c in range(0, COLS_GRID, 2)])

    held, up, down = upper
    letters = {"h": held, "u": up, "d": down}
    own = jnp.stack([pick_by(z, [letters[c] for c in table]) for table in (FROM_0, FROM_1)])
    by_x = [
        lax.ppermute(own, "prow", [(r, (r + d * NZ) % ROWS_GRID) for r in range(ROWS_GRID)]) for d in range(1, NX)
    ]

    current = pl.pallas_call(
        schur_kernel,
        out_shape=like(LR, LC, B, B),
        in_specs=[smem()] + [anywhere()] * 9,
        out_specs=anywhere(),
        scratch_shapes=[
            pltpu.VMEM((2, UCAP, B, B), BF16),
            pltpu.VMEM((2, LR, B, B), BF16),
            pltpu.VMEM((LC, LR, B, B), BF16),
            pltpu.SemaphoreType.DMA((NX,)),
            pltpu.SemaphoreType.DMA((2,)),
            pltpu.SemaphoreType.DMA((LC,)),
            pltpu.SemaphoreType.DMA((LC,)),
        ],
        input_output_aliases={9: 0},
        compiler_params=params(24),
        cost_estimate=cost(2 * LR * 12 * B**3, 90 * block),
        name="schur",
    )(block_pattern, own, *by_x, lower0_even, lower0_odd, lower1_even, lower1_odd, current)
    return jnp.transpose(current, (0, 2, 1, 3)).reshape(matrix.shape)


def solution(mesh):
    placed = (P("prow", None, None, "pcol", None, None), P("prow", None, None), P())
    return jax.shard_map(
        local,
        mesh=mesh,
        in_specs=placed,
        out_specs=P("prow", None, None, "pcol", None, None),
        check_vma=False,
    )
```

time: 509 us -> 90.9 us (0.18)
  the two profiles are of different devices: /device:TPU:2 before, /device:TPU:96 now
where the time goes in v1:
time: 90.9 us; the launch traced here: 89.8 us
  starting transfers between devices  41.3 us (45%)
  waiting for transfers between devices  22.3 us (25%)
  Pallas kernels  14.4 us (16%)
  local copies, waits for them, and re-layouts  10.9 us (12%)
    ppermute x2, starting transfers between devices, spread(): up = lax.ppermute(held, axes, along_z(NEAR_UP, cols))  13.8 us
    unnamed x13, local copies, waits for them, and re-layouts  10.8 us
    ppermute x3, waiting for transfers between devices, local(): lax.ppermute(own, 'prow', [(r, (r + d * NZ) % ROWS_GRID) for r in range(R...  8.78 us
    ppermute x2, waiting for transfers between devices, spread(): far_up = lax.ppermute(mine, axes, along_z(FAR_UP, cols))  7.06 us
    ppermute x6, waiting for transfers between devices, along_y(): lax.ppermute(lower, 'pcol', [(core, 2 * d + core)])  6.48 us
    ppermute x6, starting transfers between devices, along_y(): lax.ppermute(lower, 'pcol', [(core, 2 * d + core)])  6 us
    pallas_call x1, Pallas kernels, local(): pl.pallas_call(permute_kernel, out_shape=like(LR, LC, B, B), grid=(LR,),...  5.96 us
    ppermute x3, starting transfers between devices, local(): lax.ppermute(own, 'prow', [(r, (r + d * NZ) % ROWS_GRID) for r in range(R...  5.45 us
  transfers between devices with their start and end apart: 26, of which 4 were waited for; matrix products, arithmetic and copies ran while one was open for 1% of the time, Pallas kernels for 9%

profile of v1, /device:TPU:96, one launch (start us, length us, event | category | flops | bytes accessed | tf_op | source)
XLA Modules:
  0.0 89.8 jit_solution(4458010665725044164)
XLA Ops:
  0.0 0.7 copy.8
  0.7 2.3 %copy-done.2 = bf16[1,3,256,1,12,256]{5,2,4,3,1,0:T(8,128)(2,1)S(1)} copy-done((bf16[1,3,256,1,12,256]{5,2,4,3,1,0:T(8,128)(2,1)S(1)}, bf16[1,3,256,1,12,256]{5,2,4,3,1,0:T(8,128)(2,1)}, u32[]{:S(2)}) %copy-start.2) | copy-done | bytes 4718616
  3.0 0.8 copy-done.4
  3.8 1.9 %pack.1 = (bf16[4,6,64,256]{3,2,1,0:T(8,128)(2,1)S(1)}, bf16[256,256]{1,0:T(8,128)(2,1)S(1)}) custom-call(s32[96,96]{1,0:T(8,128)S(1)} %copy-done.4, s32[3,256]{1,0:T(4,128)S(1)} %bitcast.29, bf16[3,12,256,256]{3,2,1,0:T(8,128)(2,1)S(1)} %bitcast.27), custom_call_target="tpu_custom_call" | custom-call | flops 234881024 | bytes 2490368 | tf_op jit(solution)/shard_map/pack/pallas_call | solution.py:311
  9.2 2.3 %copy-done.3 = bf16[1,3,256,1,12,256]{5,2,4,3,1,0:T(8,128)(2,1)S(1)} copy-done((bf16[1,3,256,1,12,256]{5,2,4,3,1,0:T(8,128)(2,1)S(1)}, bf16[1,3,256,1,12,256]{5,2,4,3,1,0:T(8,128)(2,1)}, u32[]{:S(2)}) %copy-start.3) | copy-done | bytes 4718616
  11.5 6.0 %permute.1.column_ref.in_ref = bf16[3,12,256,256]{3,2,1,0:T(8,128)(2,1)} custom-call(s32[96,96]{1,0:T(8,128)S(1)} %copy-done.5, s32[3,256]{1,0:T(4,128)S(1)} %bitcast.30, bf16[3,12,256,256]{3,2,1,0:T(8,128)(2,1)S(1)} %bitcast.28), custom_call_target="tpu_custom_call" | custom-call | flops 1207959552 | bytes 9437184 | tf_op jit(solution)/shard_map/permute/pallas_call | solution.py:326
  18.2 1.3 %collective-permute-start.14 = (bf16[256,256]{1,0:T(8,128)(2,1)S(1)}, bf16[256,256]{1,0:T(8,128)(2,1)S(1)}, u32[]{:S(2)}, u32[]{:S(2)}) collective-permute-start(bf16[256,256]{1,0:T(8,128)(2,1)S(1)} %select_select_fusion.6), channel_id=1, source_target_pairs={{0,24},{1,25},{8,32},{9,33},{64,88},{65,89},{72,96},{73,97},{128,1... | collective-permute-start | bytes 393224 | tf_op jit(solution)/shard_map/ppermute | solution.py:271
  20.3 1.3 %collective-permute-start.4 = (bf16[6,64,256]{2,1,0:T(8,128)(2,1)S(1)}, bf16[6,64,256]{2,1,0:T(8,128)(2,1)S(1)}, u32[]{:S(2)}, u32[]{:S(2)}) collective-permute-start(bf16[6,64,256]{2,1,0:T(8,128)(2,1)S(1)} %fusion.1), channel_id=1, source_target_pairs={{0,24},{8,32},{64,88},{72,96},{128,152},{136,160},{192,216},{200,2... | collective-permute-start | bytes 589832 | tf_op jit(solution)/shard_map/ppermute | solution.py:271
  22.3 7.1 %collective-permute-done.14 = bf16[256,256]{1,0:T(8,128)(2,1)S(1)} collective-permute-done((bf16[256,256]{1,0:T(8,128)(2,1)S(1)}, bf16[256,256]{1,0:T(8,128)(2,1)S(1)}, u32[]{:S(2)}, u32[]{:S(2)}) %collective-permute-start.14) | collective-permute-done | bytes 131104 | tf_op jit(solution)/shard_map/ppermute | solution.py:271
  29.4 1.9 %collective-permute-start.16 = (bf16[256,256]{1,0:T(8,128)(2,1)S(1)}, bf16[256,256]{1,0:T(8,128)(2,1)S(1)}, u32[]{:S(2)}, u32[]{:S(2)}) collective-permute-start(bf16[256,256]{1,0:T(8,128)(2,1)S(1)} %select_select_fusion.4.held_ref), channel_id=1, source_target_pairs={{0,56},{1,57},{24,16},{25,17},{8,0},{9,1},{32,24},{33,25},{64,120}... | collective-permute-start | bytes 393224 | tf_op jit(solution)/shard_map/ppermute | solution.py:275
  31.3 10.9 %collective-permute-start.15 = (bf16[256,256]{1,0:T(8,128)(2,1)S(1)}, bf16[256,256]{1,0:T(8,128)(2,1)S(1)}, u32[]{:S(2)}, u32[]{:S(2)}) collective-permute-start(bf16[256,256]{1,0:T(8,128)(2,1)S(1)} %select_select_fusion.4.held_ref), channel_id=1, source_target_pairs={{0,8},{1,9},{24,32},{25,33},{40,48},{41,49},{8,16},{9,17},{32,40},... | collective-permute-start | bytes 393224 | tf_op jit(solution)/shard_map/ppermute | solution.py:274
  42.3 2.8 %collective-permute-start.6 = (bf16[6,64,256]{2,1,0:T(8,128)(2,1)S(1)}, bf16[6,64,256]{2,1,0:T(8,128)(2,1)S(1)}, u32[]{:S(2)}, u32[]{:S(2)}) collective-permute-start(bf16[6,64,256]{2,1,0:T(8,128)(2,1)S(1)} %select_select_fusion.2), channel_id=1, source_target_pairs={{0,8},{24,32},{40,48},{8,16},{32,40},{48,56},{64,72},{88,96},{104,... | collective-permute-start | bytes 589832 | tf_op jit(solution)/shard_map/ppermute | solution.py:274
  45.2 1.9 %collective-permute-start.5 = (bf16[6,64,256]{2,1,0:T(8,128)(2,1)S(1)}, bf16[6,64,256]{2,1,0:T(8,128)(2,1)S(1)}, u32[]{:S(2)}, u32[]{:S(2)}) collective-permute-start(bf16[6,64,256]{2,1,0:T(8,128)(2,1)S(1)} %select_select_fusion.2), channel_id=1, source_target_pairs={{0,56},{24,16},{8,0},{32,24},{64,120},{88,80},{72,64},{96,88},{128... | collective-permute-start | bytes 589832 | tf_op jit(solution)/shard_map/ppermute | solution.py:275
  47.1 2.3 %copy-done = bf16[3,12,256,256]{3,2,1,0:T(8,128)(2,1)S(1)} copy-done((bf16[3,12,256,256]{3,2,1,0:T(8,128)(2,1)S(1)}, bf16[3,12,256,256]{3,2,1,0:T(8,128)(2,1)}, u32[]{:S(2)}) %copy-start) | copy-done | bytes 4718616
  49.5 1.9 %inverse.1 = (bf16[3,256,256]{2,1,0:T(8,128)(2,1)S(1)}, bf16[256,256]{1,0:T(8,128)(2,1)S(1)}, bf16[256,256]{1,0:T(8,128)(2,1)S(1)}, bf16[256,256]{1,0:T(8,128)(2,1)S(1)}) custom-call(bf16[256,256]{1,0:T(8,128)(2,1)S(1)} %select_select_fusion.4.held_ref, bf16[256,256]{1,0:T(8,128)(2,1)S(1)} %collective-permute-done.15.up_ref, ...), custom_call_target="tpu_custom_call" | custom-call | flops 603979776 | bytes 1572864 | tf_op jit(solution)/shard_map/inverse/pallas_call | solution.py:337
  51.4 1.6 %collective-permute-start.21 = (bf16[3,256,256]{2,1,0:T(8,128)(2,1)S(1)}, bf16[3,256,256]{2,1,0:T(8,128)(2,1)S(1)}, u32[]{:S(2)}, u32[]{:S(2)}) collective-permute-start(bf16[3,256,256]{2,1,0:T(8,128)(2,1)S(1)} %get-tuple-element.13), channel_id=1, source_target_pairs={{0,1},{8,9},{16,17},{24,25},{32,33},{40,41},{48,49},{56,57},{64,65... | collective-permute-start | bytes 1179656 | tf_op jit(solution)/shard_map/ppermute | solution.py:348
  53.0 1.3 %collective-permute-start.19 = (bf16[3,256,256]{2,1,0:T(8,128)(2,1)S(1)}, bf16[3,256,256]{2,1,0:T(8,128)(2,1)S(1)}, u32[]{:S(2)}, u32[]{:S(2)}) collective-permute-start(bf16[3,256,256]{2,1,0:T(8,128)(2,1)S(1)} %get-tuple-element.13), channel_id=1, source_target_pairs={{0,2},{8,10},{16,18},{24,26},{32,34},{40,42},{48,50},{56,58},{64,6... | collective-permute-start | bytes 1179656 | tf_op jit(solution)/shard_map/ppermute | solution.py:361
  54.4 1.3 %collective-permute-start.18 = (bf16[3,256,256]{2,1,0:T(8,128)(2,1)S(1)}, bf16[3,256,256]{2,1,0:T(8,128)(2,1)S(1)}, u32[]{:S(2)}, u32[]{:S(2)}) collective-permute-start(bf16[3,256,256]{2,1,0:T(8,128)(2,1)S(1)} %get-tuple-element.13), channel_id=1, source_target_pairs={{0,4},{8,12},{16,20},{24,28},{32,36},{40,44},{48,52},{56,60},{64,6... | collective-permute-start | bytes 1179656 | tf_op jit(solution)/shard_map/ppermute | solution.py:361
  55.7 1.3 %collective-permute-start.17 = (bf16[3,256,256]{2,1,0:T(8,128)(2,1)S(1)}, bf16[3,256,256]{2,1,0:T(8,128)(2,1)S(1)}, u32[]{:S(2)}, u32[]{:S(2)}) collective-permute-start(bf16[3,256,256]{2,1,0:T(8,128)(2,1)S(1)} %get-tuple-element.13), channel_id=1, source_target_pairs={{0,6},{8,14},{16,22},{24,30},{32,38},{40,46},{48,54},{56,62},{64,7... | collective-permute-start | bytes 1179656 | tf_op jit(solution)/shard_map/ppermute | solution.py:361
  57.2 2.3 %copy-done.1 = bf16[3,12,256,256]{3,2,1,0:T(8,128)(2,1)S(1)} copy-done((bf16[3,12,256,256]{3,2,1,0:T(8,128)(2,1)S(1)}, bf16[3,12,256,256]{3,2,1,0:T(8,128)(2,1)}, u32[]{:S(2)}) %copy-start.1) | copy-done | bytes 4718616
  59.5 0.7 collective-permute-start.24
  60.2 0.7 collective-permute-start.23
  60.9 0.7 collective-permute-start.22
  61.7 6.5 %collective-permute-done.18 = bf16[3,256,256]{2,1,0:T(8,128)(2,1)S(1)} collective-permute-done((bf16[3,256,256]{2,1,0:T(8,128)(2,1)S(1)}, bf16[3,256,256]{2,1,0:T(8,128)(2,1)S(1)}, u32[]{:S(2)}, u32[]{:S(2)}) %collective-permute-start.18) | collective-permute-done | bytes 393248 | tf_op jit(solution)/shard_map/ppermute | solution.py:361
  68.1 2.6 %collective-permute-start.9 = (bf16[2,6,64,256]{3,2,1,0:T(8,128)(2,1)S(1)}, bf16[2,6,64,256]{3,2,1,0:T(8,128)(2,1)S(1)}, u32[]{:S(2)}, u32[]{:S(2)}) collective-permute-start(bf16[2,6,64,256]{3,2,1,0:T(8,128)(2,1)S(1)} %pad_maximum_fusion.own_ref), channel_id=1, source_target_pairs={{0,192},{8,200},{16,208},{24,216},{32,224},{40,232},{48,240},{56,2... | collective-permute-start | bytes 1179656 | tf_op jit(solution)/shard_map/ppermute | solution.py:373
  70.7 1.3 %collective-permute-start.8 = (bf16[2,6,64,256]{3,2,1,0:T(8,128)(2,1)S(1)}, bf16[2,6,64,256]{3,2,1,0:T(8,128)(2,1)S(1)}, u32[]{:S(2)}, u32[]{:S(2)}) collective-permute-start(bf16[2,6,64,256]{3,2,1,0:T(8,128)(2,1)S(1)} %pad_maximum_fusion.own_ref), channel_id=1, source_target_pairs={{0,128},{8,136},{16,144},{24,152},{32,160},{40,168},{48,176},{56,1... | collective-permute-start | bytes 1179656 | tf_op jit(solution)/shard_map/ppermute | solution.py:373
  72.2 1.5 %collective-permute-start.7 = (bf16[2,6,64,256]{3,2,1,0:T(8,128)(2,1)S(1)}, bf16[2,6,64,256]{3,2,1,0:T(8,128)(2,1)S(1)}, u32[]{:S(2)}, u32[]{:S(2)}) collective-permute-start(bf16[2,6,64,256]{3,2,1,0:T(8,128)(2,1)S(1)} %pad_maximum_fusion.own_ref), channel_id=1, source_target_pairs={{0,64},{8,72},{16,80},{24,88},{32,96},{40,104},{48,112},{56,120},{... | collective-permute-start | bytes 1179656 | tf_op jit(solution)/shard_map/ppermute | solution.py:373
  73.7 1.3 %collective-permute-start.20 = (bf16[3,256,256]{2,1,0:T(8,128)(2,1)S(1)}, bf16[3,256,256]{2,1,0:T(8,128)(2,1)S(1)}, u32[]{:S(2)}, u32[]{:S(2)}) collective-permute-start(bf16[3,256,256]{2,1,0:T(8,128)(2,1)S(1)} %select_select_fusion.1.low0e_ref), channel_id=1, source_target_pairs={{0,1},{2,3},{4,5},{6,7},{8,9},{10,11},{12,13},{14,15},{16,17},{18,... | collective-permute-start | bytes 1179656 | tf_op jit(solution)/shard_map/ppermute | solution.py:365
  75.1 1.3 %collective-permute-start.25 = (bf16[3,256,256]{2,1,0:T(8,128)(2,1)S(1)}, bf16[3,256,256]{2,1,0:T(8,128)(2,1)S(1)}, u32[]{:S(2)}, u32[]{:S(2)}) collective-permute-start(bf16[3,256,256]{2,1,0:T(8,128)(2,1)S(1)} %select_select_fusion.low1o_ref), channel_id=1, source_target_pairs={{1,0},{3,2},{5,4},{7,6},{9,8},{11,10},{13,12},{15,14},{17,16},{19,... | collective-permute-start | bytes 1179656 | tf_op jit(solution)/shard_map/ppermute | solution.py:367
  76.4 5.1 %collective-permute-done.9.three_ref = bf16[2,6,64,256]{3,2,1,0:T(8,128)(2,1)S(1)} collective-permute-done((bf16[2,6,64,256]{3,2,1,0:T(8,128)(2,1)S(1)}, bf16[2,6,64,256]{3,2,1,0:T(8,128)(2,1)S(1)}, u32[]{:S(2)}, u32[]{:S(2)}) %collective-permute-start.9) | collective-permute-done | bytes 393248 | tf_op jit(solution)/shard_map/ppermute | solution.py:373
  81.5 3.7 %collective-permute-done.7.one_ref = bf16[2,6,64,256]{3,2,1,0:T(8,128)(2,1)S(1)} collective-permute-done((bf16[2,6,64,256]{3,2,1,0:T(8,128)(2,1)S(1)}, bf16[2,6,64,256]{3,2,1,0:T(8,128)(2,1)S(1)}, u32[]{:S(2)}, u32[]{:S(2)}) %collective-permute-start.7) | collective-permute-done | bytes 393248 | tf_op jit(solution)/shard_map/ppermute | solution.py:373
  85.2 4.7 %schur.1 = bf16[3,12,256,256]{3,2,1,0:T(8,128)(2,1)} custom-call(s32[96,96]{1,0:T(8,128)S(1)} %copy-done.5, bf16[2,6,64,256]{3,2,1,0:T(8,128)(2,1)S(1)} %pad_maximum_fusion.own_ref, bf16[2,6,64,256]{3,2,1,0:T(8,128)(2,1)S(1)} %collective-permute-done.7.one_ref, ...), custom_call_target="tpu_custom_call", output_to_operand_aliasing={{}: (9, {})} | custom-call | flops 1207959552 | bytes 11796480 | tf_op jit(solution)/shard_map/schur/pallas_call | solution.py:376
  (47 shorter events, 6.0 us)
Async XLA Ops:
  0.7 2.3 %copy-start.2 = (bf16[1,3,256,1,12,256]{5,2,4,3,1,0:T(8,128)(2,1)S(1)}, bf16[1,3,256,1,12,256]{5,2,4,3,1,0:T(8,128)(2,1)}, u32[]{:S(2)}) copy-start(bf16[1,3,256,1,12,256]{5,2,4,3,1,0:T(8,128)(2,1)} %param.3) | copy-start | bytes 14155780
  3.0 0.8 copy-start.4
  3.8 5.4 %copy-start.5 = (s32[96,96]{1,0:T(8,128)S(1)}, s32[96,96]{1,0:T(8,128)}, u32[]{:S(2)}) copy-start(s32[96,96]{1,0:T(8,128)} %pattern_ref.5) | copy-start | bytes 110596
  5.7 11.8 %collective-permute-start.12 = (bf16[256,256]{1,0:T(8,128)(2,1)S(1)}, bf16[256,256]{1,0:T(8,128)(2,1)S(1)}, u32[]{:S(2)}, u32[]{:S(2)}) collective-permute-start(bf16[256,256]{1,0:T(8,128)(2,1)S(1)} %get-tuple-element.12), channel_id=1, source_target_pairs={{0,64},{1,65},{8,72},{9,73}} | collective-permute-start | bytes 393224 | tf_op jit(solution)/shard_map/ppermute | solution.py:269
  6.4 11.8 %collective-permute-start.11 = (bf16[256,256]{1,0:T(8,128)(2,1)S(1)}, bf16[256,256]{1,0:T(8,128)(2,1)S(1)}, u32[]{:S(2)}, u32[]{:S(2)}) collective-permute-start(bf16[256,256]{1,0:T(8,128)(2,1)S(1)} %get-tuple-element.12), channel_id=1, source_target_pairs={{0,128},{1,129},{8,136},{9,137}} | collective-permute-start | bytes 393224 | tf_op jit(solution)/shard_map/ppermute | solution.py:269
  7.1 11.1 %collective-permute-start.10 = (bf16[256,256]{1,0:T(8,128)(2,1)S(1)}, bf16[256,256]{1,0:T(8,128)(2,1)S(1)}, u32[]{:S(2)}, u32[]{:S(2)}) collective-permute-start(bf16[256,256]{1,0:T(8,128)(2,1)S(1)} %get-tuple-element.12), channel_id=1, source_target_pairs={{0,192},{1,193},{8,200},{9,201}} | collective-permute-start | bytes 393224 | tf_op jit(solution)/shard_map/ppermute | solution.py:269
  7.8 12.4 %collective-permute-start.2 = (bf16[6,64,256]{2,1,0:T(8,128)(2,1)S(1)}, bf16[6,64,256]{2,1,0:T(8,128)(2,1)S(1)}, u32[]{:S(2)}, u32[]{:S(2)}) collective-permute-start(bf16[6,64,256]{2,1,0:T(8,128)(2,1)S(1)} %get-tuple-element.17), channel_id=1, source_target_pairs={{0,64},{8,72},{1,65},{9,73},{2,66},{10,74},{3,67},{11,75},{4,68},{... | collective-permute-start | bytes 589832 | tf_op jit(solution)/shard_map/ppermute | solution.py:269
  8.5 11.8 %collective-permute-start.1 = (bf16[6,64,256]{2,1,0:T(8,128)(2,1)S(1)}, bf16[6,64,256]{2,1,0:T(8,128)(2,1)S(1)}, u32[]{:S(2)}, u32[]{:S(2)}) collective-permute-start(bf16[6,64,256]{2,1,0:T(8,128)(2,1)S(1)} %get-tuple-element.18), channel_id=1, source_target_pairs={{0,128},{8,136},{1,129},{9,137},{2,130},{10,138},{3,131},{11,139},... | collective-permute-start | bytes 589832 | tf_op jit(solution)/shard_map/ppermute | solution.py:269
  9.2 2.3 %copy-start.3 = (bf16[1,3,256,1,12,256]{5,2,4,3,1,0:T(8,128)(2,1)S(1)}, bf16[1,3,256,1,12,256]{5,2,4,3,1,0:T(8,128)(2,1)}, u32[]{:S(2)}) copy-start(bf16[1,3,256,1,12,256]{5,2,4,3,1,0:T(8,128)(2,1)} %param.3) | copy-start | bytes 14155780
  17.5 2.7 %collective-permute-start = (bf16[6,64,256]{2,1,0:T(8,128)(2,1)S(1)}, bf16[6,64,256]{2,1,0:T(8,128)(2,1)S(1)}, u32[]{:S(2)}, u32[]{:S(2)}) collective-permute-start(bf16[6,64,256]{2,1,0:T(8,128)(2,1)S(1)} %get-tuple-element.19), channel_id=1, source_target_pairs={{0,192},{8,200},{1,193},{9,201},{2,194},{10,202},{3,195},{11,203},... | collective-permute-start | bytes 589832 | tf_op jit(solution)/shard_map/ppermute | solution.py:269
  18.2 11.1 %collective-permute-start.14 = (bf16[256,256]{1,0:T(8,128)(2,1)S(1)}, bf16[256,256]{1,0:T(8,128)(2,1)S(1)}, u32[]{:S(2)}, u32[]{:S(2)}) collective-permute-start(bf16[256,256]{1,0:T(8,128)(2,1)S(1)} %select_select_fusion.6), channel_id=1, source_target_pairs={{0,24},{1,25},{8,32},{9,33},{64,88},{65,89},{72,96},{73,97},{128,1... | collective-permute-start | bytes 393224 | tf_op jit(solution)/shard_map/ppermute | solution.py:271
  19.5 9.8 %collective-permute-start.13 = (bf16[256,256]{1,0:T(8,128)(2,1)S(1)}, bf16[256,256]{1,0:T(8,128)(2,1)S(1)}, u32[]{:S(2)}, u32[]{:S(2)}) collective-permute-start(bf16[256,256]{1,0:T(8,128)(2,1)S(1)} %select_select_fusion.6), channel_id=1, source_target_pairs={{0,40},{1,41},{8,48},{9,49},{64,104},{65,105},{72,112},{73,113},{1... | collective-permute-start | bytes 393224 | tf_op jit(solution)/shard_map/ppermute | solution.py:272
  20.3 22.0 %collective-permute-start.4 = (bf16[6,64,256]{2,1,0:T(8,128)(2,1)S(1)}, bf16[6,64,256]{2,1,0:T(8,128)(2,1)S(1)}, u32[]{:S(2)}, u32[]{:S(2)}) collective-permute-start(bf16[6,64,256]{2,1,0:T(8,128)(2,1)S(1)} %fusion.1), channel_id=1, source_target_pairs={{0,24},{8,32},{64,88},{72,96},{128,152},{136,160},{192,216},{200,2... | collective-permute-start | bytes 589832 | tf_op jit(solution)/shard_map/ppermute | solution.py:271
  21.6 20.7 %collective-permute-start.3 = (bf16[6,64,256]{2,1,0:T(8,128)(2,1)S(1)}, bf16[6,64,256]{2,1,0:T(8,128)(2,1)S(1)}, u32[]{:S(2)}, u32[]{:S(2)}) collective-permute-start(bf16[6,64,256]{2,1,0:T(8,128)(2,1)S(1)} %fusion.1), channel_id=1, source_target_pairs={{0,40},{8,48},{64,104},{72,112},{128,168},{136,176},{192,232},{200... | collective-permute-start | bytes 589832 | tf_op jit(solution)/shard_map/ppermute | solution.py:272
  29.4 17.7 %collective-permute-start.16 = (bf16[256,256]{1,0:T(8,128)(2,1)S(1)}, bf16[256,256]{1,0:T(8,128)(2,1)S(1)}, u32[]{:S(2)}, u32[]{:S(2)}) collective-permute-start(bf16[256,256]{1,0:T(8,128)(2,1)S(1)} %select_select_fusion.4.held_ref), channel_id=1, source_target_pairs={{0,56},{1,57},{24,16},{25,17},{8,0},{9,1},{32,24},{33,25},{64,120}... | collective-permute-start | bytes 393224 | tf_op jit(solution)/shard_map/ppermute | solution.py:275
  31.3 15.8 %collective-permute-start.15 = (bf16[256,256]{1,0:T(8,128)(2,1)S(1)}, bf16[256,256]{1,0:T(8,128)(2,1)S(1)}, u32[]{:S(2)}, u32[]{:S(2)}) collective-permute-start(bf16[256,256]{1,0:T(8,128)(2,1)S(1)} %select_select_fusion.4.held_ref), channel_id=1, source_target_pairs={{0,8},{1,9},{24,32},{25,33},{40,48},{41,49},{8,16},{9,17},{32,40},... | collective-permute-start | bytes 393224 | tf_op jit(solution)/shard_map/ppermute | solution.py:274
  42.3 13.4 %collective-permute-start.6 = (bf16[6,64,256]{2,1,0:T(8,128)(2,1)S(1)}, bf16[6,64,256]{2,1,0:T(8,128)(2,1)S(1)}, u32[]{:S(2)}, u32[]{:S(2)}) collective-permute-start(bf16[6,64,256]{2,1,0:T(8,128)(2,1)S(1)} %select_select_fusion.2), channel_id=1, source_target_pairs={{0,8},{24,32},{40,48},{8,16},{32,40},{48,56},{64,72},{88,96},{104,... | collective-permute-start | bytes 589832 | tf_op jit(solution)/shard_map/ppermute | solution.py:274
  45.2 11.9 %collective-permute-start.5 = (bf16[6,64,256]{2,1,0:T(8,128)(2,1)S(1)}, bf16[6,64,256]{2,1,0:T(8,128)(2,1)S(1)}, u32[]{:S(2)}, u32[]{:S(2)}) collective-permute-start(bf16[6,64,256]{2,1,0:T(8,128)(2,1)S(1)} %select_select_fusion.2), channel_id=1, source_target_pairs={{0,56},{24,16},{8,0},{32,24},{64,120},{88,80},{72,64},{96,88},{128... | collective-permute-start | bytes 589832 | tf_op jit(solution)/shard_map/ppermute | solution.py:275
  47.1 2.3 %copy-start = (bf16[3,12,256,256]{3,2,1,0:T(8,128)(2,1)S(1)}, bf16[3,12,256,256]{3,2,1,0:T(8,128)(2,1)}, u32[]{:S(2)}) copy-start(bf16[3,12,256,256]{3,2,1,0:T(8,128)(2,1)} %permute.1.column_ref.in_ref) | copy-start | bytes 14155780
  51.4 5.8 %collective-permute-start.21 = (bf16[3,256,256]{2,1,0:T(8,128)(2,1)S(1)}, bf16[3,256,256]{2,1,0:T(8,128)(2,1)S(1)}, u32[]{:S(2)}, u32[]{:S(2)}) collective-permute-start(bf16[3,256,256]{2,1,0:T(8,128)(2,1)S(1)} %get-tuple-element.13), channel_id=1, source_target_pairs={{0,1},{8,9},{16,17},{24,25},{32,33},{40,41},{48,49},{56,57},{64,65... | collective-permute-start | bytes 1179656 | tf_op jit(solution)/shard_map/ppermute | solution.py:348
  53.0 7.9 %collective-permute-start.19 = (bf16[3,256,256]{2,1,0:T(8,128)(2,1)S(1)}, bf16[3,256,256]{2,1,0:T(8,128)(2,1)S(1)}, u32[]{:S(2)}, u32[]{:S(2)}) collective-permute-start(bf16[3,256,256]{2,1,0:T(8,128)(2,1)S(1)} %get-tuple-element.13), channel_id=1, source_target_pairs={{0,2},{8,10},{16,18},{24,26},{32,34},{40,42},{48,50},{56,58},{64,6... | collective-permute-start | bytes 1179656 | tf_op jit(solution)/shard_map/ppermute | solution.py:361
  54.4 13.8 %collective-permute-start.18 = (bf16[3,256,256]{2,1,0:T(8,128)(2,1)S(1)}, bf16[3,256,256]{2,1,0:T(8,128)(2,1)S(1)}, u32[]{:S(2)}, u32[]{:S(2)}) collective-permute-start(bf16[3,256,256]{2,1,0:T(8,128)(2,1)S(1)} %get-tuple-element.13), channel_id=1, source_target_pairs={{0,4},{8,12},{16,20},{24,28},{32,36},{40,44},{48,52},{56,60},{64,6... | collective-permute-start | bytes 1179656 | tf_op jit(solution)/shard_map/ppermute | solution.py:361
  55.7 15.0 %collective-permute-start.17 = (bf16[3,256,256]{2,1,0:T(8,128)(2,1)S(1)}, bf16[3,256,256]{2,1,0:T(8,128)(2,1)S(1)}, u32[]{:S(2)}, u32[]{:S(2)}) collective-permute-start(bf16[3,256,256]{2,1,0:T(8,128)(2,1)S(1)} %get-tuple-element.13), channel_id=1, source_target_pairs={{0,6},{8,14},{16,22},{24,30},{32,38},{40,46},{48,54},{56,62},{64,7... | collective-permute-start | bytes 1179656 | tf_op jit(solution)/shard_map/ppermute | solution.py:361
  57.2 2.3 %copy-start.1 = (bf16[3,12,256,256]{3,2,1,0:T(8,128)(2,1)S(1)}, bf16[3,12,256,256]{3,2,1,0:T(8,128)(2,1)}, u32[]{:S(2)}) copy-start(bf16[3,12,256,256]{3,2,1,0:T(8,128)(2,1)} %permute.1.column_ref.in_ref) | copy-start | bytes 14155780
  59.5 12.6 %collective-permute-start.24 = (bf16[3,256,256]{2,1,0:T(8,128)(2,1)S(1)}, bf16[3,256,256]{2,1,0:T(8,128)(2,1)S(1)}, u32[]{:S(2)}, u32[]{:S(2)}) collective-permute-start(bf16[3,256,256]{2,1,0:T(8,128)(2,1)S(1)} %second.1), channel_id=1, source_target_pairs={{1,3},{9,11},{17,19},{25,27},{33,35},{41,43},{49,51},{57,59},{65,6... | collective-permute-start | bytes 1179656 | tf_op jit(solution)/shard_map/ppermute | solution.py:361
  60.2 13.5 %collective-permute-start.23 = (bf16[3,256,256]{2,1,0:T(8,128)(2,1)S(1)}, bf16[3,256,256]{2,1,0:T(8,128)(2,1)S(1)}, u32[]{:S(2)}, u32[]{:S(2)}) collective-permute-start(bf16[3,256,256]{2,1,0:T(8,128)(2,1)S(1)} %second.1), channel_id=1, source_target_pairs={{1,5},{9,13},{17,21},{25,29},{33,37},{41,45},{49,53},{57,61},{65,6... | collective-permute-start | bytes 1179656 | tf_op jit(solution)/shard_map/ppermute | solution.py:361
  60.9 14.1 %collective-permute-start.22 = (bf16[3,256,256]{2,1,0:T(8,128)(2,1)S(1)}, bf16[3,256,256]{2,1,0:T(8,128)(2,1)S(1)}, u32[]{:S(2)}, u32[]{:S(2)}) collective-permute-start(bf16[3,256,256]{2,1,0:T(8,128)(2,1)S(1)} %second.1), channel_id=1, source_target_pairs={{1,7},{9,15},{17,23},{25,31},{33,39},{41,47},{49,55},{57,63},{65,7... | collective-permute-start | bytes 1179656 | tf_op jit(solution)/shard_map/ppermute | solution.py:361
  68.1 13.3 %collective-permute-start.9 = (bf16[2,6,64,256]{3,2,1,0:T(8,128)(2,1)S(1)}, bf16[2,6,64,256]{3,2,1,0:T(8,128)(2,1)S(1)}, u32[]{:S(2)}, u32[]{:S(2)}) collective-permute-start(bf16[2,6,64,256]{3,2,1,0:T(8,128)(2,1)S(1)} %pad_maximum_fusion.own_ref), channel_id=1, source_target_pairs={{0,192},{8,200},{16,208},{24,216},{32,224},{40,232},{48,240},{56,2... | collective-permute-start | bytes 1179656 | tf_op jit(solution)/shard_map/ppermute | solution.py:373
  70.7 10.7 %collective-permute-start.8 = (bf16[2,6,64,256]{3,2,1,0:T(8,128)(2,1)S(1)}, bf16[2,6,64,256]{3,2,1,0:T(8,128)(2,1)S(1)}, u32[]{:S(2)}, u32[]{:S(2)}) collective-permute-start(bf16[2,6,64,256]{3,2,1,0:T(8,128)(2,1)S(1)} %pad_maximum_fusion.own_ref), channel_id=1, source_target_pairs={{0,128},{8,136},{16,144},{24,152},{32,160},{40,168},{48,176},{56,1... | collective-permute-start | bytes 1179656 | tf_op jit(solution)/shard_map/ppermute | solution.py:373
  72.2 13.0 %collective-permute-start.7 = (bf16[2,6,64,256]{3,2,1,0:T(8,128)(2,1)S(1)}, bf16[2,6,64,256]{3,2,1,0:T(8,128)(2,1)S(1)}, u32[]{:S(2)}, u32[]{:S(2)}) collective-permute-start(bf16[2,6,64,256]{3,2,1,0:T(8,128)(2,1)S(1)} %pad_maximum_fusion.own_ref), channel_id=1, source_target_pairs={{0,64},{8,72},{16,80},{24,88},{32,96},{40,104},{48,112},{56,120},{... | collective-permute-start | bytes 1179656 | tf_op jit(solution)/shard_map/ppermute | solution.py:373
  73.7 11.5 %collective-permute-start.20 = (bf16[3,256,256]{2,1,0:T(8,128)(2,1)S(1)}, bf16[3,256,256]{2,1,0:T(8,128)(2,1)S(1)}, u32[]{:S(2)}, u32[]{:S(2)}) collective-permute-start(bf16[3,256,256]{2,1,0:T(8,128)(2,1)S(1)} %select_select_fusion.1.low0e_ref), channel_id=1, source_target_pairs={{0,1},{2,3},{4,5},{6,7},{8,9},{10,11},{12,13},{14,15},{16,17},{18,... | collective-permute-start | bytes 1179656 | tf_op jit(solution)/shard_map/ppermute | solution.py:365
  75.1 10.1 %collective-permute-start.25 = (bf16[3,256,256]{2,1,0:T(8,128)(2,1)S(1)}, bf16[3,256,256]{2,1,0:T(8,128)(2,1)S(1)}, u32[]{:S(2)}, u32[]{:S(2)}) collective-permute-start(bf16[3,256,256]{2,1,0:T(8,128)(2,1)S(1)} %select_select_fusion.low1o_ref), channel_id=1, source_target_pairs={{1,0},{3,2},{5,4},{7,6},{9,8},{11,10},{13,12},{15,14},{17,16},{19,... | collective-permute-start | bytes 1179656 | tf_op jit(solution)/shard_map/ppermute | solution.py:367

commit v2 on v1

v2 whole, which is shorter than its diff:
```python
import functools

import jax
import jax.numpy as jnp
from jax import lax
from jax.experimental import pallas as pl
from jax.experimental.pallas import tpu as pltpu
from jax.sharding import PartitionSpec as P

B = 256
LR = 3
LC = 12
NB = 96
UCAP = 6
NEWTON = 3
ROWS_GRID = 32
COLS_GRID = 8
NX = 4
NZ = 8
PIECE = B // NX
SELECT_BYTES = 8 << 20
MIB = 1 << 20

F32 = jnp.float32
BF16 = jnp.bfloat16

FAR_UP = [(0, 3), (1, 4)]
FAR_DOWN = [(0, 5), (1, 6)]
NEAR_UP = [(0, 1), (3, 4), (5, 6), (1, 2), (4, 5), (6, 7)]
NEAR_DOWN = [(0, 7), (3, 2), (1, 0), (4, 3)]
FROM_0 = "hudhuhud"
FROM_1 = "dhudhuhu"
SKIPS = (2, -2, 4)
SKIP_OF = (0, 0, 1, 1, 3, 3, 2, 2)
HELD_ROW = (0, 1) * (NZ // 2)


def skip_z(skip):
    return [(z, (z + skip) % NZ) for z in range(2)]


def ring_z(step):
    return [(z, (z + step) % NZ) for z in range(NZ)]


def one_hot_rows(order):
    source = lax.broadcasted_iota(jnp.int32, (B, B), 0)
    return jnp.where(source == order, 1.0, 0.0).T.astype(BF16)


def split(value, parts):
    out = []
    for _ in range(parts):
        head = value.astype(BF16)
        out.append(head)
        value = value - head.astype(F32)
    return out


def dot(a, b):
    return jnp.dot(a, b, preferred_element_type=F32)


def pack_kernel(pattern_hbm, order_hbm, blocks_hbm, packed_ref, first_ref, pattern, order, blocks, sem, block_sem):
    small = [
        pltpu.make_async_copy(order_hbm.at[0], order, sem.at[0]),
        pltpu.make_async_copy(pattern_hbm.at[0:8], pattern, sem.at[1]),
    ]
    fetches = [pltpu.make_async_copy(blocks_hbm.at[0, u], blocks.at[u], block_sem.at[u]) for u in range(LC)]
    for copy in small + fetches:
        copy.start()
    for copy in small:
        copy.wait()
    supernode = jnp.minimum(lax.axis_index("prow"), 1)
    grid_col = lax.axis_index("pcol")
    pick = one_hot_rows(order[...])
    slot = jnp.int32(0)
    chosen = [jnp.int32(0)] * UCAP
    for u in range(LC):
        col = grid_col + u * COLS_GRID
        used = (pattern[supernode, col] != 0) & (col > supernode)
        chosen = [jnp.where(used & (slot == s), u, c) for s, c in enumerate(chosen)]
        slot = slot + used.astype(jnp.int32)
    for copy in fetches:
        copy.wait()
    present = pattern[supernode, grid_col] != 0
    first_ref[...] = jnp.where(present, dot(pick, blocks[0]), 0.0).astype(BF16)
    for s, u in enumerate(chosen):
        block = dot(pick, blocks[u]).astype(BF16)
        for piece in range(NX):
            packed_ref[piece, s] = block[piece * PIECE : (piece + 1) * PIECE]


def permute_kernel(t, pattern_hbm, order_hbm, blocks_hbm, after, placed_ref, pattern, order, blocks, sem, block_sem):
    del after
    row = t * ROWS_GRID + lax.axis_index("prow")
    grid_col = lax.axis_index("pcol")
    small = [
        pltpu.make_async_copy(order_hbm.at[t], order, sem.at[0]),
        pltpu.make_async_copy(pattern_hbm.at[pl.ds(pl.multiple_of(row // 8 * 8, 8), 8)], pattern, sem.at[1]),
    ]
    fetches = [pltpu.make_async_copy(blocks_hbm.at[t, u], blocks.at[u], block_sem.at[u]) for u in range(LC)]
    for copy in small + fetches:
        copy.start()
    for copy in small:
        copy.wait()
    pick = one_hot_rows(order[...])
    for copy in fetches:
        copy.wait()
    for u in range(LC):
        present = pattern[row % 8, grid_col + u * COLS_GRID] != 0
        placed_ref[u] = jnp.where(present, dot(pick, blocks[u]), 0.0).astype(BF16)


def select_kernel(choices, *refs):
    *options, out_ref = refs
    part, table = choices
    grid_row = lax.axis_index("prow")
    place = {"x": grid_row // NZ, "z": grid_row % NZ, "y": lax.axis_index("pcol") // 2}[part]
    for i in range(max(table) + 1):
        hit = functools.reduce(jnp.logical_or, [place == p for p, choice in enumerate(table) if choice == i])

        @pl.when(hit)
        def _(i=i):
            out_ref[...] = options[i][...]


def inverse_kernel(
    held_ref, up_ref, down_ref, pattern_hbm, order_hbm, blocks_hbm, after,
    lower_ref, first_ref, high_ref, low_ref, column_ref,
    pattern, orders, blocks, sem, pattern_sem,
):
    del after
    grid_row = lax.axis_index("prow")
    grid_col = lax.axis_index("pcol")
    z = grid_row % NZ

    def chosen(table):
        def of(letter, ref):
            hit = functools.reduce(jnp.logical_or, [z == i for i in range(NZ) if table[i] == letter])
            return hit, ref

        (held, h), (up, u) = of("h", held_ref), of("u", up_ref)
        return jnp.where(
            held, h[...].astype(F32), jnp.where(up, u[...].astype(F32), down_ref[...].astype(F32))
        )

    @pl.when(grid_col < 2)
    def _():
        fetches = [
            pltpu.make_async_copy(order_hbm, orders, sem.at[0]),
            pltpu.make_async_copy(blocks_hbm.at[:, 0], blocks, sem.at[1]),
        ]
        for t in range(LR):
            group = pl.ds(pl.multiple_of((t * ROWS_GRID + grid_row) // 8 * 8, 8), 8)
            fetches.append(pltpu.make_async_copy(pattern_hbm.at[group], pattern.at[t], pattern_sem.at[t]))
        for copy in fetches:
            copy.start()
        first = chosen(FROM_0)
        first_ref[...] = first.astype(BF16)
        block = jnp.where(grid_col == 0, first, chosen(FROM_1))
        diagonal = lax.broadcasted_iota(jnp.int32, (B, B), 0) == lax.broadcasted_iota(jnp.int32, (B, B), 1)
        pivots = jnp.where(diagonal, block, 0.0)
        by_col = 1.0 / jnp.sum(pivots, axis=0, keepdims=True)
        by_row = 1.0 / jnp.sum(pivots, axis=1, keepdims=True)
        twice = jnp.where(diagonal, 2.0, 0.0)
        inverse = by_row * (twice - block * by_col)
        block16 = block.astype(BF16)
        for _ in range(NEWTON - 1):
            high, middle, low = split(inverse, 3)
            rest = twice - (dot(block16, high) + (dot(block16, middle) + dot(block16, low)))
            rest_high, rest_low = split(rest, 2)
            inverse = dot(high, rest_high) + (dot(high, rest_low) + dot(middle, rest_high))
        high, low = split(inverse, 2)
        high_ref[...] = high
        low_ref[...] = low
        for copy in fetches:
            copy.wait()
        for t in range(LR):
            present = pattern[t, grid_row % 8, grid_col] != 0
            column = jnp.where(present, dot(one_hot_rows(orders[t]), blocks[t]), 0.0).astype(BF16)
            column_ref[t] = column
            lower = dot(column, high) + dot(column, low)
            lower_ref[t] = jnp.where(t * ROWS_GRID + grid_row > 0, lower, 0.0).astype(BF16)


def second_kernel(own_ref, lower_ref, first_ref, high_ref, low_ref, column_ref, out_ref):
    grid_row = lax.axis_index("prow")

    @pl.when(lax.axis_index("pcol") == 0)
    def _():
        out_ref[...] = own_ref[...]

    @pl.when(lax.axis_index("pcol") == 1)
    def _():
        for t in range(LR):
            rest = (column_ref[t].astype(F32) - dot(lower_ref[t], first_ref[...])).astype(BF16)
            lower = dot(rest, high_ref[...]) + dot(rest, low_ref[...])
            out_ref[t] = jnp.where(t * ROWS_GRID + grid_row > 1, lower, 0.0).astype(BF16)


def schur_kernel(
    pattern_hbm, held0, held1, held2, held3, other01, other23, mine_ref, neighbour_ref, row0, row1, row2,
    out_hbm, pattern, upper, lower, work, sem, upper_sem, lower_sem, out_sem,
):
    rows = (row0, row1, row2)
    grid_row = lax.axis_index("prow")
    grid_col = lax.axis_index("pcol")
    x, z = grid_row // NZ, grid_row % NZ
    held_row = functools.reduce(jnp.logical_or, [z == i for i in range(NZ) if HELD_ROW[i]]).astype(jnp.int32)

    def plan(u):
        col = grid_col + u * COLS_GRID
        use0 = (pattern[0, col] != 0) & (col > 0)
        use1 = (pattern[1, col] != 0) & (col > 1)
        return use0, use1, use0 | use1 | (col < 2)

    def store(u):
        return pltpu.make_async_copy(work.at[u], out_hbm.at[:, u], out_sem.at[u])

    def passed(u):
        return [pltpu.make_async_copy(rows[t].at[u], out_hbm.at[t, u], out_sem.at[u]) for t in range(LR)]

    rows_of = pltpu.make_async_copy(pattern_hbm.at[0:8], pattern, sem)
    rows_of.start()
    operands = [
        pltpu.make_async_copy(mine_ref, lower.at[grid_col % 2], lower_sem.at[0]),
        pltpu.make_async_copy(neighbour_ref, lower.at[1 - grid_col % 2], lower_sem.at[1]),
    ]
    for k, refs in ((held_row, (held0, held1, held2, held3)), (1 - held_row, [pair.at[i] for pair in (other01, other23) for i in range(2)])):
        for shift, ref in enumerate(refs):
            part = pl.ds(pl.multiple_of((x + NX - shift) % NX * PIECE, PIECE), PIECE)
            operands.append(pltpu.make_async_copy(ref, upper.at[k, :, part, :], upper_sem.at[len(operands)]))
    for copy in operands:
        copy.start()
    rows_of.wait()

    def start_passed(u, carry):
        @pl.when(jnp.logical_not(plan(u)[2]))
        def _():
            for copy in passed(u):
                copy.start()

        return carry

    lax.fori_loop(0, LC, start_passed, 0)
    for copy in operands:
        copy.wait()

    def step(u, slots):
        use0, use1, touched = plan(u)
        slot0, slot1 = slots

        @pl.when(touched)
        def _():
            for t in range(LR):
                work[u, t] = rows[t][u]

            def update(k, slot):
                product = dot(lower[k].reshape(LR * B, B), upper[k, slot]).reshape(LR, B, B)
                work[u] = (work[u].astype(F32) - product).astype(BF16)

            @pl.when(use0)
            def _():
                update(0, slot0)

            @pl.when(use1)
            def _():
                update(1, slot1)

            for k in range(2):

                @pl.when((u == 0) & (grid_col == k))
                def _(k=k):
                    for t in range(LR):

                        @pl.when(t * ROWS_GRID + grid_row > k)
                        def _(t=t):
                            work[0, t] = lower[k, t]

            store(u).start()

        return slot0 + use0.astype(jnp.int32), slot1 + use1.astype(jnp.int32)

    lax.fori_loop(0, LC, step, (jnp.int32(0), jnp.int32(0)))

    def finish(u, carry):
        store(u).wait()
        return carry

    lax.fori_loop(0, LC, finish, 0)


def pick_by(index, options):
    value = None
    for i, option in enumerate(options):
        if option is not None:
            value = option if value is None else jnp.where(index == i, option, value)
    return value


def along_z(pairs, cols):
    rows = [(x * NZ + a, x * NZ + b) for x in range(NX) for a, b in pairs]
    if cols is None:
        return rows
    return [(a * COLS_GRID + c, b * COLS_GRID + c) for a, b in rows for c in cols]


def from_x0(shift, cols):
    rows = [(z, shift * NZ + z) for z in range(2)]
    if cols is None:
        return rows
    return [(a * COLS_GRID + c, b * COLS_GRID + c) for a, b in rows for c in cols]


def scattered(sent, cols):
    axes = "prow" if cols is None else ("prow", "pcol")
    return [sent[0]] + [lax.ppermute(sent[d], axes, from_x0(d, cols)) for d in range(1, NX)]


def select(part, table, *options, after=()):
    return pl.pallas_call(
        functools.partial(select_kernel, (part, tuple(table))),
        out_shape=jax.ShapeDtypeStruct(options[0].shape, options[0].dtype),
        in_specs=[vmem()] * len(options) + [anywhere()] * len(after),
        out_specs=vmem(),
        compiler_params=params(8),
        cost_estimate=cost(0, SELECT_BYTES),
        name="select",
    )(*options, *after)


def spread_whole(first, x, cols, after):
    axes = ("prow", "pcol")
    mine = pick_by(x, scattered([first] * NX, cols))
    far_up = lax.ppermute(mine, axes, along_z(FAR_UP, cols))
    far_down = lax.ppermute(mine, axes, along_z(FAR_DOWN, cols))
    held = select("z", (0, 0, 0, 1, 1, 2, 2, 0), mine, far_up, far_down, after=after)
    up = lax.ppermute(held, axes, along_z(NEAR_UP, cols))
    down = lax.ppermute(held, axes, along_z(NEAR_DOWN, cols))
    return held, up, down


def gather_x(own):
    shifted = [[(r, (r + d * NZ) % ROWS_GRID) for r in range(ROWS_GRID)] for d in range(1, NX)]
    return [own] + [lax.ppermute(own, "prow", pairs) for pairs in shifted]


def vmem():
    return pl.BlockSpec(memory_space=pltpu.VMEM)


def hbm():
    return pl.BlockSpec(memory_space=pltpu.HBM)


def in_hbm(value):
    return pltpu.with_memory_space_constraint(value, pltpu.HBM)


def anywhere():
    return pl.BlockSpec(memory_space=pl.ANY)


def like(*shape):
    return jax.ShapeDtypeStruct(shape, BF16)


def params(limit):
    return pltpu.CompilerParams(vmem_limit_bytes=limit * MIB)


def cost(flops, moved):
    return pl.CostEstimate(flops=flops, bytes_accessed=moved, transcendentals=0)


def local(matrix, row_perm, block_pattern):
    grid_row = lax.axis_index("prow")
    grid_col = lax.axis_index("pcol")
    x, z = grid_row // NZ, grid_row % NZ
    blocks = in_hbm(jnp.transpose(matrix[0, :, :, 0], (0, 2, 1, 3)))
    orders = in_hbm(row_perm.reshape(LR, 1, B))
    block_pattern = in_hbm(block_pattern)
    block = B * B * 2
    small_scratch = [pltpu.SMEM((8, NB), jnp.int32), pltpu.VMEM((1, B), jnp.int32)]
    dma = pltpu.SemaphoreType.DMA

    def permute(t, after):
        return pl.pallas_call(
            functools.partial(permute_kernel, t),
            out_shape=pltpu.VMEM((LC, B, B), BF16),
            in_specs=[hbm()] * 3 + [anywhere()],
            out_specs=vmem(),
            scratch_shapes=small_scratch + [pltpu.VMEM((LC, B, B), BF16), dma((2,)), dma((LC,))],
            compiler_params=params(16),
            cost_estimate=cost(2 * LC * B**3, 2 * LC * block),
            name="permute",
        )(block_pattern, orders, blocks, after)

    packed, first = pl.pallas_call(
        pack_kernel,
        out_shape=(like(NX, UCAP, PIECE, B), like(B, B)),
        in_specs=[hbm(), hbm(), hbm()],
        out_specs=(vmem(), vmem()),
        scratch_shapes=small_scratch + [pltpu.VMEM((LC, B, B), BF16), dma((2,)), dma((LC,))],
        compiler_params=params(16),
        cost_estimate=cost(2 * 7 * B**3, 19 * block),
        name="pack",
    )(block_pattern, orders, blocks)

    mine = select("x", range(NX), *scattered([packed[d] for d in range(NX)], None))
    held, up, down = spread_whole(first, x, (0, 1), (mine,))
    skipped = [lax.ppermute(mine, "prow", along_z(skip_z(skip), None)) for skip in SKIPS]
    placed = [permute(0, held)]
    held_row = select("z", SKIP_OF, mine, *skipped, after=placed)
    held_rows = gather_x(held_row)
    other_rows = [
        lax.ppermute(jnp.stack(held_rows[i : i + 2]), "prow", along_z(ring_z(step), None)) for i, step in ((0, 1), (2, -1))
    ]

    lower0, first0, high, low, column = pl.pallas_call(
        inverse_kernel,
        out_shape=(like(LR, B, B), like(B, B), like(B, B), like(B, B), like(LR, B, B)),
        in_specs=[vmem(), vmem(), vmem(), hbm(), hbm(), hbm(), anywhere()],
        out_specs=(vmem(),) * 5,
        scratch_shapes=[
            pltpu.SMEM((LR, 8, NB), jnp.int32),
            pltpu.VMEM((LR, 1, B), jnp.int32),
            pltpu.VMEM((LR, B, B), BF16),
            dma((2,)),
            dma((LR,)),
        ],
        compiler_params=params(16),
        cost_estimate=cost(2 * 18 * B**3, 12 * block),
        name="inverse",
    )(held, up, down, block_pattern, orders, blocks, held_row)

    neighbour0 = lax.ppermute(lower0, "pcol", [(0, 1)])
    lower = pl.pallas_call(
        second_kernel,
        out_shape=like(LR, B, B),
        in_specs=[vmem()] * 6,
        out_specs=vmem(),
        compiler_params=params(16),
        cost_estimate=cost(2 * 9 * B**3, 12 * block),
        name="second",
    )(lower0, neighbour0, first0, high, low, column)

    placed += [permute(t, lower) for t in range(1, LR)]
    got = [lax.ppermute(lower, "pcol", [(0, 2 * d), (1, 2 * d + 1)]) for d in range(1, COLS_GRID // 2)]
    lower_mine = select("y", range(4), lower, *got, after=placed[1:])
    lower_neighbour = lax.ppermute(lower_mine, "pcol", [(c, c ^ 1) for c in range(COLS_GRID)])

    current = pl.pallas_call(
        schur_kernel,
        out_shape=like(LR, LC, B, B),
        in_specs=[hbm()] + [anywhere()] * (NX + 4) + [vmem()] * LR,
        out_specs=hbm(),
        scratch_shapes=[
            pltpu.SMEM((8, NB), jnp.int32),
            pltpu.VMEM((2, UCAP, B, B), BF16),
            pltpu.VMEM((2, LR, B, B), BF16),
            pltpu.VMEM((LC, LR, B, B), BF16),
            dma,
            dma((2 * NX + 2,)),
            dma((2,)),
            dma((LC,)),
        ],
        compiler_params=params(24),
        cost_estimate=cost(2 * LR * 12 * B**3, 90 * block),
        name="schur",
    )(block_pattern, *held_rows, *other_rows, lower_mine, lower_neighbour, *placed)
    return jnp.transpose(current, (0, 2, 1, 3)).reshape(matrix.shape)


def solution(mesh):
    placed = (P("prow", None, None, "pcol", None, None), P("prow", None, None), P())
    return jax.shard_map(
        local,
        mesh=mesh,
        in_specs=placed,
        out_specs=P("prow", None, None, "pcol", None, None),
        check_vma=False,
    )
```

time: 90.9 us -> 73.6 us (0.81)
  the two profiles are of different devices: /device:TPU:96 before, /device:TPU:14 now
where the time goes in v2:
time: 73.6 us; the launch traced here: 73.3 us
  waiting for transfers between devices  32.6 us (44%)
  starting transfers between devices  26.8 us (36%)
  Pallas kernels  13.3 us (18%)
    ppermute x3, waiting for transfers between devices, local(): lax.ppermute(lower, 'pcol', [(0, 2 * d), (1, 2 * d + 1)])  14.5 us
    ppermute x3, starting transfers between devices, gather_x(): return [own] + [lax.ppermute(own, 'prow', pairs) for pairs in shifted]  8.36 us
    ppermute x3, waiting for transfers between devices, local(): lax.ppermute(mine, 'prow', along_z(skip_z(skip), None))  6.81 us
    pallas_call x3, Pallas kernels, permute(): pl.pallas_call(functools.partial(permute_kernel, t), out_shape=pltpu.VMEM...  6.44 us
    ppermute x6, waiting for transfers between devices, scattered(): lax.ppermute(sent[d], axes, from_x0(d, cols))  5.66 us
    ppermute x3, starting transfers between devices, local(): lax.ppermute(mine, 'prow', along_z(skip_z(skip), None))  5.5 us
    pallas_call x1, Pallas kernels, local(): pl.pallas_call(schur_kernel, out_shape=like(LR, LC, B, B), in_specs=[hbm(...  4.76 us
    ppermute x6, starting transfers between devices, scattered(): lax.ppermute(sent[d], axes, from_x0(d, cols))  4.65 us
  transfers between devices with their start and end apart: 23, of which 5 were waited for; matrix products, arithmetic and copies ran while one was open for 0% of the time, Pallas kernels for 9%

profile of v2, /device:TPU:14, one launch (start us, length us, event | category | flops | bytes accessed | tf_op | source)
XLA Modules:
  0.0 73.3 jit_solution(11704887252897150185)
XLA Ops:
  0.0 2.0 %pack.1 = (bf16[4,6,64,256]{3,2,1,0:T(8,128)(2,1)S(1)}, bf16[256,256]{1,0:T(8,128)(2,1)S(1)}) custom-call(s32[96,96]{1,0:T(8,128)} %pattern_hbm.11, s32[3,1,256]{2,1,0:T(1,128)} %bitcast.30, bf16[3,12,256,256]{3,2,1,0:T(8,128)(2,1)} %bitcast.25), custom_call_target="tpu_custom_call" | custom-call | flops 234881024 | bytes 2490368 | tf_op jit(solution)/shard_map/pack/pallas_call | solution.py:400
  2.0 0.7 collective-permute-start.8
  2.7 0.7 collective-permute-start.7
  3.3 0.7 collective-permute-start.6
  4.1 1.3 %collective-permute-start.2 = (bf16[6,64,256]{2,1,0:T(8,128)(2,1)S(1)}, bf16[6,64,256]{2,1,0:T(8,128)(2,1)S(1)}, u32[]{:S(2)}, u32[]{:S(2)}) collective-permute-start(bf16[6,64,256]{2,1,0:T(8,128)(2,1)S(1)} %get-tuple-element.19), channel_id=1, source_target_pairs={{0,192},{8,200},{1,193},{9,201},{2,194},{10,202},{3,195},{11,203},... | collective-permute-start | bytes 589832 | tf_op jit(solution)/shard_map/ppermute | solution.py:318
  5.4 0.7 collective-permute-start.1
  6.1 0.7 collective-permute-start
  6.8 0.7 collective-permute-start.10
  7.5 0.7 collective-permute-start.9
  8.2 5.6 %collective-permute-done.2.refs_3_ = bf16[6,64,256]{2,1,0:T(8,128)(2,1)S(1)} collective-permute-done((bf16[6,64,256]{2,1,0:T(8,128)(2,1)S(1)}, bf16[6,64,256]{2,1,0:T(8,128)(2,1)S(1)}, u32[]{:S(2)}, u32[]{:S(2)}) %collective-permute-start.2) | collective-permute-done | bytes 196640 | tf_op jit(solution)/shard_map/ppermute | solution.py:318
  13.8 2.9 %collective-permute-start.5 = (bf16[6,64,256]{2,1,0:T(8,128)(2,1)S(1)}, bf16[6,64,256]{2,1,0:T(8,128)(2,1)S(1)}, u32[]{:S(2)}, u32[]{:S(2)}) collective-permute-start(bf16[6,64,256]{2,1,0:T(8,128)(2,1)S(1)} %select.8.refs_3_.refs_0_), channel_id=1, source_target_pairs={{0,32},{8,40},{64,96},{72,104},{128,160},{136,168},{192,224},{200,... | collective-permute-start | bytes 589832 | tf_op jit(solution)/shard_map/ppermute | solution.py:413
  16.8 1.3 %collective-permute-start.4 = (bf16[6,64,256]{2,1,0:T(8,128)(2,1)S(1)}, bf16[6,64,256]{2,1,0:T(8,128)(2,1)S(1)}, u32[]{:S(2)}, u32[]{:S(2)}) collective-permute-start(bf16[6,64,256]{2,1,0:T(8,128)(2,1)S(1)} %select.8.refs_3_.refs_0_), channel_id=1, source_target_pairs={{0,48},{8,56},{64,112},{72,120},{128,176},{136,184},{192,240},{200... | collective-permute-start | bytes 589832 | tf_op jit(solution)/shard_map/ppermute | solution.py:413
  18.1 1.3 %collective-permute-start.3 = (bf16[6,64,256]{2,1,0:T(8,128)(2,1)S(1)}, bf16[6,64,256]{2,1,0:T(8,128)(2,1)S(1)}, u32[]{:S(2)}, u32[]{:S(2)}) collective-permute-start(bf16[6,64,256]{2,1,0:T(8,128)(2,1)S(1)} %select.8.refs_3_.refs_0_), channel_id=1, source_target_pairs={{0,16},{8,24},{64,80},{72,88},{128,144},{136,152},{192,208},{200,2... | collective-permute-start | bytes 589832 | tf_op jit(solution)/shard_map/ppermute | solution.py:413
  19.4 0.7 collective-permute-start.17
  20.1 0.7 collective-permute-start.16
  20.8 2.1 %permute.3.refs_4_.row0 = bf16[12,256,256]{2,1,0:T(8,128)(2,1)S(1)} custom-call(s32[96,96]{1,0:T(8,128)} %pattern_hbm.11, s32[3,1,256]{2,1,0:T(1,128)} %bitcast.31, bf16[3,12,256,256]{3,2,1,0:T(8,128)(2,1)} %bitcast.26, bf16[256,256]{1,0:T(8,128)(2,1)S(1)} %select.9.after.held_ref), custom_call_target="tpu_custom_call" | custom-call | flops 402653184 | bytes 3145728 | tf_op jit(solution)/shard_map/permute/pallas_call | solution.py:389
  23.0 6.8 %collective-permute-done.4.refs_2_ = bf16[6,64,256]{2,1,0:T(8,128)(2,1)S(1)} collective-permute-done((bf16[6,64,256]{2,1,0:T(8,128)(2,1)S(1)}, bf16[6,64,256]{2,1,0:T(8,128)(2,1)S(1)}, u32[]{:S(2)}, u32[]{:S(2)}) %collective-permute-start.4) | collective-permute-done | bytes 196640 | tf_op jit(solution)/shard_map/ppermute | solution.py:413
  29.9 0.7 collective-permute-start.18
  30.6 1.0 %collective-permute-start.13 = (bf16[6,64,256]{2,1,0:T(8,128)(2,1)S(1)}, bf16[6,64,256]{2,1,0:T(8,128)(2,1)S(1)}, u32[]{:S(2)}, u32[]{:S(2)}) collective-permute-start(bf16[6,64,256]{2,1,0:T(8,128)(2,1)S(1)} %select.10.after.held0), channel_id=1, source_target_pairs={{0,192},{8,200},{16,208},{24,216},{32,224},{40,232},{48,240},{56,2... | collective-permute-start | bytes 589832 | tf_op jit(solution)/shard_map/ppermute | solution.py:346
  31.5 4.9 %collective-permute-start.12 = (bf16[6,64,256]{2,1,0:T(8,128)(2,1)S(1)}, bf16[6,64,256]{2,1,0:T(8,128)(2,1)S(1)}, u32[]{:S(2)}, u32[]{:S(2)}) collective-permute-start(bf16[6,64,256]{2,1,0:T(8,128)(2,1)S(1)} %select.10.after.held0), channel_id=1, source_target_pairs={{0,128},{8,136},{16,144},{24,152},{32,160},{40,168},{48,176},{56,1... | collective-permute-start | bytes 589832 | tf_op jit(solution)/shard_map/ppermute | solution.py:346
  36.4 2.5 %collective-permute-start.11 = (bf16[6,64,256]{2,1,0:T(8,128)(2,1)S(1)}, bf16[6,64,256]{2,1,0:T(8,128)(2,1)S(1)}, u32[]{:S(2)}, u32[]{:S(2)}) collective-permute-start(bf16[6,64,256]{2,1,0:T(8,128)(2,1)S(1)} %select.10.after.held0), channel_id=1, source_target_pairs={{0,64},{8,72},{16,80},{24,88},{32,96},{40,104},{48,112},{56,120},{... | collective-permute-start | bytes 589832 | tf_op jit(solution)/shard_map/ppermute | solution.py:346
  39.0 0.7 collective-permute-start.21
  39.6 0.7 collective-permute-start.20
  40.3 1.3 %collective-permute-start.19 = (bf16[3,256,256]{2,1,0:T(8,128)(2,1)S(1)}, bf16[3,256,256]{2,1,0:T(8,128)(2,1)S(1)}, u32[]{:S(2)}, u32[]{:S(2)}) collective-permute-start(bf16[3,256,256]{2,1,0:T(8,128)(2,1)S(1)} %second.1.after.refs_0_), channel_id=1, source_target_pairs={{0,2},{1,3},{8,10},{9,11},{16,18},{17,19},{24,26},{25,27},{32,34},... | collective-permute-start | bytes 1179656 | tf_op jit(solution)/shard_map/ppermute | solution.py:450
  41.6 3.9 %collective-permute-done.12.held2 = bf16[6,64,256]{2,1,0:T(8,128)(2,1)S(1)} collective-permute-done((bf16[6,64,256]{2,1,0:T(8,128)(2,1)S(1)}, bf16[6,64,256]{2,1,0:T(8,128)(2,1)S(1)}, u32[]{:S(2)}, u32[]{:S(2)}) %collective-permute-start.12) | collective-permute-done | bytes 196640 | tf_op jit(solution)/shard_map/ppermute | solution.py:346
  45.8 2.1 %collective-permute-start.14 = (bf16[2,6,64,256]{3,2,1,0:T(8,128)(2,1)S(1)}, bf16[2,6,64,256]{3,2,1,0:T(8,128)(2,1)S(1)}, u32[]{:S(2)}, u32[]{:S(2)}) collective-permute-start(bf16[2,6,64,256]{3,2,1,0:T(8,128)(2,1)S(1)} %pad_maximum_fusion), channel_id=1, source_target_pairs={{0,8},{8,16},{16,24},{24,32},{32,40},{40,48},{48,56},{56,0},{64,72... | collective-permute-start | bytes 1179656 | tf_op jit(solution)/shard_map/ppermute | solution.py:418
  47.8 2.1 %permute.5.refs_5_.row2 = bf16[12,256,256]{2,1,0:T(8,128)(2,1)S(1)} custom-call(s32[96,96]{1,0:T(8,128)} %pattern_hbm.11, s32[3,1,256]{2,1,0:T(1,128)} %bitcast.33, bf16[3,12,256,256]{3,2,1,0:T(8,128)(2,1)} %bitcast.28, bf16[3,256,256]{2,1,0:T(8,128)(2,1)S(1)} %second.1.after.refs_0_), custom_call_target="tpu_custom_call" | custom-call | flops 402653184 | bytes 3145728 | tf_op jit(solution)/shard_map/permute/pallas_call | solution.py:389
  50.0 2.1 %permute.4.refs_4_.row1 = bf16[12,256,256]{2,1,0:T(8,128)(2,1)S(1)} custom-call(s32[96,96]{1,0:T(8,128)} %pattern_hbm.11, s32[3,1,256]{2,1,0:T(1,128)} %bitcast.34, bf16[3,12,256,256]{3,2,1,0:T(8,128)(2,1)} %bitcast.29, bf16[3,256,256]{2,1,0:T(8,128)(2,1)S(1)} %second.1.after.refs_0_), custom_call_target="tpu_custom_call" | custom-call | flops 402653184 | bytes 3145728 | tf_op jit(solution)/shard_map/permute/pallas_call | solution.py:389
  52.2 14.5 %collective-permute-done.19.refs_1_ = bf16[3,256,256]{2,1,0:T(8,128)(2,1)S(1)} collective-permute-done((bf16[3,256,256]{2,1,0:T(8,128)(2,1)S(1)}, bf16[3,256,256]{2,1,0:T(8,128)(2,1)S(1)}, u32[]{:S(2)}, u32[]{:S(2)}) %collective-permute-start.19) | collective-permute-done | bytes 393248 | tf_op jit(solution)/shard_map/ppermute | solution.py:450
  66.7 0.1 collective-permute-start.22
  66.8 1.7 %collective-permute-done.22.neighbour_ref = bf16[3,256,256]{2,1,0:T(8,128)(2,1)S(1)} collective-permute-done((bf16[3,256,256]{2,1,0:T(8,128)(2,1)S(1)}, bf16[3,256,256]{2,1,0:T(8,128)(2,1)S(1)}, u32[]{:S(2)}, u32[]{:S(2)}) %collective-permute-start.22) | collective-permute-done | bytes 393248 | tf_op jit(solution)/shard_map/ppermute | solution.py:452
  68.5 4.8 %schur.1 = bf16[3,12,256,256]{3,2,1,0:T(8,128)(2,1)} custom-call(s32[96,96]{1,0:T(8,128)} %pattern_hbm.11, bf16[6,64,256]{2,1,0:T(8,128)(2,1)S(1)} %select.10.after.held0, bf16[6,64,256]{2,1,0:T(8,128)(2,1)S(1)} %collective-permute-done.11.held1, bf16[6,64,256]{2,1,0:T(8,128)(2,1)S(1)} %collective-permute-done.12.held2, ...), custom_call_target="tpu_custom_call" | custom-call | flops 1207959552 | bytes 11796480 | tf_op jit(solution)/shard_map/schur/pallas_call | solution.py:454
  (29 shorter events, 0.5 us)
Async XLA Ops:
  2.0 4.1 %collective-permute-start.8 = (bf16[256,256]{1,0:T(8,128)(2,1)S(1)}, bf16[256,256]{1,0:T(8,128)(2,1)S(1)}, u32[]{:S(2)}, u32[]{:S(2)}) collective-permute-start(bf16[256,256]{1,0:T(8,128)(2,1)S(1)} %get-tuple-element.13), channel_id=1, source_target_pairs={{0,64},{1,65},{8,72},{9,73}} | collective-permute-start | bytes 393224 | tf_op jit(solution)/shard_map/ppermute | solution.py:318
  2.7 4.1 %collective-permute-start.7 = (bf16[256,256]{1,0:T(8,128)(2,1)S(1)}, bf16[256,256]{1,0:T(8,128)(2,1)S(1)}, u32[]{:S(2)}, u32[]{:S(2)}) collective-permute-start(bf16[256,256]{1,0:T(8,128)(2,1)S(1)} %get-tuple-element.13), channel_id=1, source_target_pairs={{0,128},{1,129},{8,136},{9,137}} | collective-permute-start | bytes 393224 | tf_op jit(solution)/shard_map/ppermute | solution.py:318
  3.3 3.4 %collective-permute-start.6 = (bf16[256,256]{1,0:T(8,128)(2,1)S(1)}, bf16[256,256]{1,0:T(8,128)(2,1)S(1)}, u32[]{:S(2)}, u32[]{:S(2)}) collective-permute-start(bf16[256,256]{1,0:T(8,128)(2,1)S(1)} %get-tuple-element.13), channel_id=1, source_target_pairs={{0,192},{1,193},{8,200},{9,201}} | collective-permute-start | bytes 393224 | tf_op jit(solution)/shard_map/ppermute | solution.py:318
  4.1 9.7 %collective-permute-start.2 = (bf16[6,64,256]{2,1,0:T(8,128)(2,1)S(1)}, bf16[6,64,256]{2,1,0:T(8,128)(2,1)S(1)}, u32[]{:S(2)}, u32[]{:S(2)}) collective-permute-start(bf16[6,64,256]{2,1,0:T(8,128)(2,1)S(1)} %get-tuple-element.19), channel_id=1, source_target_pairs={{0,192},{8,200},{1,193},{9,201},{2,194},{10,202},{3,195},{11,203},... | collective-permute-start | bytes 589832 | tf_op jit(solution)/shard_map/ppermute | solution.py:318
  5.4 8.4 %collective-permute-start.1 = (bf16[6,64,256]{2,1,0:T(8,128)(2,1)S(1)}, bf16[6,64,256]{2,1,0:T(8,128)(2,1)S(1)}, u32[]{:S(2)}, u32[]{:S(2)}) collective-permute-start(bf16[6,64,256]{2,1,0:T(8,128)(2,1)S(1)} %get-tuple-element.20), channel_id=1, source_target_pairs={{0,128},{8,136},{1,129},{9,137},{2,130},{10,138},{3,131},{11,139},... | collective-permute-start | bytes 589832 | tf_op jit(solution)/shard_map/ppermute | solution.py:318
  6.1 7.7 %collective-permute-start = (bf16[6,64,256]{2,1,0:T(8,128)(2,1)S(1)}, bf16[6,64,256]{2,1,0:T(8,128)(2,1)S(1)}, u32[]{:S(2)}, u32[]{:S(2)}) collective-permute-start(bf16[6,64,256]{2,1,0:T(8,128)(2,1)S(1)} %get-tuple-element.21), channel_id=1, source_target_pairs={{0,64},{8,72},{1,65},{9,73},{2,66},{10,74},{3,67},{11,75},{4,68},{... | collective-permute-start | bytes 589832 | tf_op jit(solution)/shard_map/ppermute | solution.py:318
  6.8 12.6 %collective-permute-start.10 = (bf16[256,256]{1,0:T(8,128)(2,1)S(1)}, bf16[256,256]{1,0:T(8,128)(2,1)S(1)}, u32[]{:S(2)}, u32[]{:S(2)}) collective-permute-start(bf16[256,256]{1,0:T(8,128)(2,1)S(1)} %select_select_fusion.refs_0_), channel_id=1, source_target_pairs={{0,40},{1,41},{8,48},{9,49},{64,104},{65,105},{72,112},{73,113},{1... | collective-permute-start | bytes 393224 | tf_op jit(solution)/shard_map/ppermute | solution.py:337
  7.5 11.9 %collective-permute-start.9 = (bf16[256,256]{1,0:T(8,128)(2,1)S(1)}, bf16[256,256]{1,0:T(8,128)(2,1)S(1)}, u32[]{:S(2)}, u32[]{:S(2)}) collective-permute-start(bf16[256,256]{1,0:T(8,128)(2,1)S(1)} %select_select_fusion.refs_0_), channel_id=1, source_target_pairs={{0,24},{1,25},{8,32},{9,33},{64,88},{65,89},{72,96},{73,97},{128,1... | collective-permute-start | bytes 393224 | tf_op jit(solution)/shard_map/ppermute | solution.py:336
  13.8 9.1 %collective-permute-start.5 = (bf16[6,64,256]{2,1,0:T(8,128)(2,1)S(1)}, bf16[6,64,256]{2,1,0:T(8,128)(2,1)S(1)}, u32[]{:S(2)}, u32[]{:S(2)}) collective-permute-start(bf16[6,64,256]{2,1,0:T(8,128)(2,1)S(1)} %select.8.refs_3_.refs_0_), channel_id=1, source_target_pairs={{0,32},{8,40},{64,96},{72,104},{128,160},{136,168},{192,224},{200,... | collective-permute-start | bytes 589832 | tf_op jit(solution)/shard_map/ppermute | solution.py:413
  16.8 13.0 %collective-permute-start.4 = (bf16[6,64,256]{2,1,0:T(8,128)(2,1)S(1)}, bf16[6,64,256]{2,1,0:T(8,128)(2,1)S(1)}, u32[]{:S(2)}, u32[]{:S(2)}) collective-permute-start(bf16[6,64,256]{2,1,0:T(8,128)(2,1)S(1)} %select.8.refs_3_.refs_0_), channel_id=1, source_target_pairs={{0,48},{8,56},{64,112},{72,120},{128,176},{136,184},{192,240},{200... | collective-permute-start | bytes 589832 | tf_op jit(solution)/shard_map/ppermute | solution.py:413
  18.1 11.7 %collective-permute-start.3 = (bf16[6,64,256]{2,1,0:T(8,128)(2,1)S(1)}, bf16[6,64,256]{2,1,0:T(8,128)(2,1)S(1)}, u32[]{:S(2)}, u32[]{:S(2)}) collective-permute-start(bf16[6,64,256]{2,1,0:T(8,128)(2,1)S(1)} %select.8.refs_3_.refs_0_), channel_id=1, source_target_pairs={{0,16},{8,24},{64,80},{72,88},{128,144},{136,152},{192,208},{200,2... | collective-permute-start | bytes 589832 | tf_op jit(solution)/shard_map/ppermute | solution.py:413
  19.4 10.4 %collective-permute-start.17 = (bf16[256,256]{1,0:T(8,128)(2,1)S(1)}, bf16[256,256]{1,0:T(8,128)(2,1)S(1)}, u32[]{:S(2)}, u32[]{:S(2)}) collective-permute-start(bf16[256,256]{1,0:T(8,128)(2,1)S(1)} %select.9.after.held_ref), channel_id=1, source_target_pairs={{0,56},{1,57},{24,16},{25,17},{8,0},{9,1},{32,24},{33,25},{64,120}... | collective-permute-start | bytes 393224 | tf_op jit(solution)/shard_map/ppermute | solution.py:340
  20.1 9.7 %collective-permute-start.16 = (bf16[256,256]{1,0:T(8,128)(2,1)S(1)}, bf16[256,256]{1,0:T(8,128)(2,1)S(1)}, u32[]{:S(2)}, u32[]{:S(2)}) collective-permute-start(bf16[256,256]{1,0:T(8,128)(2,1)S(1)} %select.9.after.held_ref), channel_id=1, source_target_pairs={{0,8},{1,9},{24,32},{25,33},{40,48},{41,49},{8,16},{9,17},{32,40},... | collective-permute-start | bytes 393224 | tf_op jit(solution)/shard_map/ppermute | solution.py:339
  29.9 9.1 %collective-permute-start.18 = (bf16[3,256,256]{2,1,0:T(8,128)(2,1)S(1)}, bf16[3,256,256]{2,1,0:T(8,128)(2,1)S(1)}, u32[]{:S(2)}, u32[]{:S(2)}) collective-permute-start(bf16[3,256,256]{2,1,0:T(8,128)(2,1)S(1)} %get-tuple-element.14.own_ref), channel_id=1, source_target_pairs={{0,1},{8,9},{16,17},{24,25},{32,33},{40,41},{48,49},{56,57},{64,65... | collective-permute-start | bytes 1179656 | tf_op jit(solution)/shard_map/ppermute | solution.py:438
  30.6 9.7 %collective-permute-start.13 = (bf16[6,64,256]{2,1,0:T(8,128)(2,1)S(1)}, bf16[6,64,256]{2,1,0:T(8,128)(2,1)S(1)}, u32[]{:S(2)}, u32[]{:S(2)}) collective-permute-start(bf16[6,64,256]{2,1,0:T(8,128)(2,1)S(1)} %select.10.after.held0), channel_id=1, source_target_pairs={{0,192},{8,200},{16,208},{24,216},{32,224},{40,232},{48,240},{56,2... | collective-permute-start | bytes 589832 | tf_op jit(solution)/shard_map/ppermute | solution.py:346
  31.5 14.0 %collective-permute-start.12 = (bf16[6,64,256]{2,1,0:T(8,128)(2,1)S(1)}, bf16[6,64,256]{2,1,0:T(8,128)(2,1)S(1)}, u32[]{:S(2)}, u32[]{:S(2)}) collective-permute-start(bf16[6,64,256]{2,1,0:T(8,128)(2,1)S(1)} %select.10.after.held0), channel_id=1, source_target_pairs={{0,128},{8,136},{16,144},{24,152},{32,160},{40,168},{48,176},{56,1... | collective-permute-start | bytes 589832 | tf_op jit(solution)/shard_map/ppermute | solution.py:346
  36.4 9.3 %collective-permute-start.11 = (bf16[6,64,256]{2,1,0:T(8,128)(2,1)S(1)}, bf16[6,64,256]{2,1,0:T(8,128)(2,1)S(1)}, u32[]{:S(2)}, u32[]{:S(2)}) collective-permute-start(bf16[6,64,256]{2,1,0:T(8,128)(2,1)S(1)} %select.10.after.held0), channel_id=1, source_target_pairs={{0,64},{8,72},{16,80},{24,88},{32,96},{40,104},{48,112},{56,120},{... | collective-permute-start | bytes 589832 | tf_op jit(solution)/shard_map/ppermute | solution.py:346
  39.0 13.2 %collective-permute-start.21 = (bf16[3,256,256]{2,1,0:T(8,128)(2,1)S(1)}, bf16[3,256,256]{2,1,0:T(8,128)(2,1)S(1)}, u32[]{:S(2)}, u32[]{:S(2)}) collective-permute-start(bf16[3,256,256]{2,1,0:T(8,128)(2,1)S(1)} %second.1.after.refs_0_), channel_id=1, source_target_pairs={{0,6},{1,7},{8,14},{9,15},{16,22},{17,23},{24,30},{25,31},{32,38},... | collective-permute-start | bytes 1179656 | tf_op jit(solution)/shard_map/ppermute | solution.py:450
  39.6 12.5 %collective-permute-start.20 = (bf16[3,256,256]{2,1,0:T(8,128)(2,1)S(1)}, bf16[3,256,256]{2,1,0:T(8,128)(2,1)S(1)}, u32[]{:S(2)}, u32[]{:S(2)}) collective-permute-start(bf16[3,256,256]{2,1,0:T(8,128)(2,1)S(1)} %second.1.after.refs_0_), channel_id=1, source_target_pairs={{0,4},{1,5},{8,12},{9,13},{16,20},{17,21},{24,28},{25,29},{32,36},... | collective-permute-start | bytes 1179656 | tf_op jit(solution)/shard_map/ppermute | solution.py:450
  40.3 26.3 %collective-permute-start.19 = (bf16[3,256,256]{2,1,0:T(8,128)(2,1)S(1)}, bf16[3,256,256]{2,1,0:T(8,128)(2,1)S(1)}, u32[]{:S(2)}, u32[]{:S(2)}) collective-permute-start(bf16[3,256,256]{2,1,0:T(8,128)(2,1)S(1)} %second.1.after.refs_0_), channel_id=1, source_target_pairs={{0,2},{1,3},{8,10},{9,11},{16,18},{17,19},{24,26},{25,27},{32,34},... | collective-permute-start | bytes 1179656 | tf_op jit(solution)/shard_map/ppermute | solution.py:450
  45.6 21.2 %collective-permute-start.15 = (bf16[2,6,64,256]{3,2,1,0:T(8,128)(2,1)S(1)}, bf16[2,6,64,256]{3,2,1,0:T(8,128)(2,1)S(1)}, u32[]{:S(2)}, u32[]{:S(2)}) collective-permute-start(bf16[2,6,64,256]{3,2,1,0:T(8,128)(2,1)S(1)} %pad_maximum_fusion.1), channel_id=1, source_target_pairs={{0,56},{8,0},{16,8},{24,16},{32,24},{40,32},{48,40},{56,48},{64,12... | collective-permute-start | bytes 1179656 | tf_op jit(solution)/shard_map/ppermute | solution.py:418
  45.8 21.1 %collective-permute-start.14 = (bf16[2,6,64,256]{3,2,1,0:T(8,128)(2,1)S(1)}, bf16[2,6,64,256]{3,2,1,0:T(8,128)(2,1)S(1)}, u32[]{:S(2)}, u32[]{:S(2)}) collective-permute-start(bf16[2,6,64,256]{3,2,1,0:T(8,128)(2,1)S(1)} %pad_maximum_fusion), channel_id=1, source_target_pairs={{0,8},{8,16},{16,24},{24,32},{32,40},{40,48},{48,56},{56,0},{64,72... | collective-permute-start | bytes 1179656 | tf_op jit(solution)/shard_map/ppermute | solution.py:418
  66.7 1.8 %collective-permute-start.22 = (bf16[3,256,256]{2,1,0:T(8,128)(2,1)S(1)}, bf16[3,256,256]{2,1,0:T(8,128)(2,1)S(1)}, u32[]{:S(2)}, u32[]{:S(2)}) collective-permute-start(bf16[3,256,256]{2,1,0:T(8,128)(2,1)S(1)} %select.11.mine_ref), channel_id=1, source_target_pairs={{0,1},{1,0},{2,3},{3,2},{4,5},{5,4},{6,7},{7,6},{8,9},{9,8},{10,11... | collective-permute-start | bytes 1179656 | tf_op jit(solution)/shard_map/ppermute | solution.py:452
